TPU v7x, 128 devices: a whole 4x4x4 slice. The times are simulated.
128 devices in a mesh: rep: 2 (over y_lo), section: 8 (over y_hi, z), tp: 8 (over x, core).
Axes of the slice: x: 4, y: 4 (y_hi: 2, y_lo: 2; y = y_hi * 2 + y_lo), z: 4, core: 2. Of those that a mesh axis runs over, the one named last changes fastest.
Arguments:
- hidden: bfloat16 [2, 8, 16, 8192], P('rep', 'section'), may hold values from -6 to 6
- gain: float32 [8, 8192], P('section'), may hold values from 0.25 to 1.75
- w_query: bfloat16 [8, 8192, 4096], P('section', None, 'tp'), may hold values from -0.0625 to 0.0625
- w_keyval: bfloat16 [2, 8, 8192, 2048], P('rep', 'section', None, 'tp'), may hold values from -0.0625 to 0.0625
- w_out: bfloat16 [8, 4096, 8192], P('section', 'tp'), may hold values from -0.09375 to 0.09375
- old_pool: bfloat16 [4096, 32, 2048], P(('rep', 'section'), None, 'tp'), may hold values from -6 to 6
- send_index: int32 [16, 16, 32], P(('rep', 'section')), may hold values from 0 to 255
- recv_slot: int32 [16, 16, 32], P(('rep', 'section')), may hold values from 0 to 256, as said below
- holder: int32 [8], P('section'), may hold values from 0 to 1
- lengths: int32 [2, 8, 16], P('rep', 'section'), may hold values from 1 to 511, as said below
Outputs:
- next_hidden: bfloat16 [2, 8, 16, 8192], P('rep', 'section')
- cache: bfloat16 [2, 8, 16, 512, 2048], P('rep', 'section', None, None, 'tp')
Inputs may be any that keep to these rules, and one draw needn't show every extreme that they name: For every owner, each of its 256 block numbers appears exactly once in recv_slot[owner]; the other entries are 256. In every owner's row one holder fills all 32 slots. `lengths`: on every section of every replica one request has 511 positions.
All inputs are finite; a program needn't handle non-finite values.
Results may differ from a plain program's by a relative error of at most 0.004.
Values may be sent and summed in bfloat16 or wider, within the bound.
A program may use at most 128 MiB of HBM per device.

v0:
```python
import jax
import jax.numpy as jnp
from jax import lax
from jax.sharding import PartitionSpec as P

QH = 32
KVH = 8
HD = 128
CTX = 512


def broadcast(value, axis, source):
    kept = jnp.where(lax.axis_index(axis) == source, value, 0).astype(value.dtype)
    return lax.psum(kept, axis)


def shifted(value, axis, by):
    devices = lax.axis_size(axis)
    return lax.ppermute(value, axis, [(i, (i + by) % devices) for i in range(devices)])


def shards(
    hidden, gain, w_query, w_keyval, w_out, old_pool, send_index, recv_slot, holder, lengths
):
    blk_rows = old_pool.shape[1]
    width = old_pool.shape[2]
    outgoing = old_pool[send_index[0]]
    arrived = lax.all_to_all(outgoing, ("rep", "section"), split_axis=0, concat_axis=0, tiled=True)
    requests = hidden.shape[2]
    context = CTX
    nblock = requests * (context // blk_rows)
    moved = jnp.zeros((nblock, blk_rows, width), jnp.bfloat16)
    moved = moved.at[recv_slot[0].reshape(-1)].set(
        arrived.reshape(-1, blk_rows, width), mode="drop"
    )
    moved = moved.reshape(requests, context, width)
    state = hidden[0, 0].astype(jnp.float32)
    scale = lax.rsqrt(jnp.mean(state * state, axis=-1, keepdims=True) + 1e-05)
    normed = (state * scale * gain[0]).astype(jnp.bfloat16)
    query = jnp.dot(normed, w_query[0], preferred_element_type=jnp.float32).astype(jnp.bfloat16)
    slab = broadcast(w_keyval[0, 0], "rep", holder[0])
    keyval = jnp.dot(normed, slab, preferred_element_type=jnp.float32).astype(jnp.bfloat16)
    length = lengths[0, 0]
    positions = jnp.arange(context, dtype=jnp.int32)
    cache = jnp.where(positions[None, :, None] == length[:, None, None], keyval[:, None, :], moved)
    kv_heads = width // (2 * HD)
    group_size = QH // KVH
    split = cache.reshape(requests, context, kv_heads, 2, HD)
    keys = split[:, :, :, 0, :]
    values = split[:, :, :, 1, :]
    heads = query.reshape(requests, kv_heads, group_size, HD)
    scores = jnp.einsum(
        "bhgd,bjhd->bhgj", heads, keys, preferred_element_type=jnp.float32
    ) * HD ** (-0.5)
    valid = positions[None, None, None, :] <= length[:, None, None, None]
    expo = jnp.where(valid, jnp.exp(jnp.where(valid, scores, 0.0)), 0.0)
    weights = (expo / jnp.sum(expo, axis=-1, keepdims=True)).astype(jnp.bfloat16)
    attended = jnp.einsum("bhgj,bjhd->bhgd", weights, values, preferred_element_type=jnp.float32)
    attended = attended.astype(jnp.bfloat16).reshape(requests, kv_heads * group_size * HD)
    update = jnp.dot(attended, w_out[0], preferred_element_type=jnp.float32)
    total = lax.psum(update, "tp")
    after = (state + total).astype(jnp.bfloat16)
    passed = shifted(after, "section", 1)
    return (passed[None, None], cache[None, None])


def solution(mesh):
    in_specs = (
        P("rep", "section", None, None),
        P("section", None),
        P("section", None, "tp"),
        P("rep", "section", None, "tp"),
        P("section", "tp", None),
        P(("rep", "section"), None, "tp"),
        P(("rep", "section"), None, None),
        P(("rep", "section"), None, None),
        P("section"),
        P("rep", "section", None),
    )
    out_specs = (P("rep", "section", None, None), P("rep", "section", None, None, "tp"))
    return jax.shard_map(shards, mesh=mesh, in_specs=in_specs, out_specs=out_specs, check_vma=False)
```

profile of v0, /device:TPU:1, one launch (start us, length us, event | category | flops | bytes accessed | tf_op | source)
XLA Modules:
  0.0 401.0 jit_solution(12261285353094148346)
XLA Ops:
  7.2 0.7 compare_select_fusion
  7.9 0.1 reshape.216
  8.0 21.8 %gather_fusion = bf16[512,32,256]{2,1,0:T(8,128)(2,1)} fusion(bf16[256,32,256]{2,1,0:T(8,128)(2,1)} %param.15, s32[1024]{0:T(1024)S(1)} %pad_clamp_fusion), kind=kCustom, calls=%fused_computation | custom fusion | bytes 16779264 | tf_op jit(solution)/shard_map/gather | solution.py:27
  29.8 8.7 %all-to-all-start = ((bf16[16,32,32,256]{3,2,1,0:T(8,128)(2,1)}), bf16[16,32,32,256]{3,2,1,0:T(8,128)(2,1)}, u32[]{:S(2)}, u32[]{:S(2)}) async-start(bf16[16,32,32,256]{3,2,1,0:T(8,128)(2,1)} %bitcast.72), calls=%async_computation | async-start | bytes 16777216 | tf_op jit(solution)/shard_map/all_to_all | solution.py:28
  38.5 0.0 all-reduce.3.cloned.1.call-start
  39.2 4.5 %select_bitcast_fusion = bf16[8192,256]{1,0:T(8,128)(2,1)} fusion(bf16[1,1,8192,256]{3,2,1,0:T(8,128)(2,1)} %param.13, pred[]{:T(512)S(6)} %eq.21), kind=kLoop, calls=%fused_computation.7 | loop fusion | flops 2097152 | bytes 8388609 | tf_op jit(solution)/shard_map/jit(_where)/select_n | solution.py:13
  43.6 0.0 copy-start.3
  43.6 0.0 copy-start
  43.6 0.0 copy-start.2
  43.6 0.0 all-reduce.3.cloned.1.call-update
  43.7 0.2 all-reduce.5.cloned.1.call-start
  43.9 0.4 copy-done.3
  44.3 0.1 reshape_squeeze.3
  44.4 0.2 copy-done
  44.6 0.2 fusion.17
  44.8 0.0 copy-done.2
  44.8 0.0 copy-start.4
  44.8 4.6 %fusion.11 = bf16[16,512]{1,0:T(8,128)(2,1)S(1)} fusion(bf16[1,8192,512]{2,1,0:T(8,128)(2,1)} %param.12, bf16[1,1,16,8192]{3,2,1,0:T(8,128)(2,1)S(1)} %copy-done, f32[8192]{0:T(1024)S(1)} %bitcast.74, f32[16]{0:T(128)S(1)} %add_rsqrt_fusion), kind=kOutput, calls=%fused_computation.18 | convolution fusion | flops 134750208 | bytes 8699968 | tf_op jit(solution)/shard_map/dot_general | solution.py:40
  49.5 0.0 copy-done.4
  49.5 0.1 iota_compare_fusion.1
  49.6 173.3 %all-reduce.3.cloned.1.call-done = bf16[8192,256]{1,0:T(8,128)(2,1)} async-done(((bf16[8192,256]{1,0:T(8,128)(2,1)}), bf16[8192,256]{1,0:T(8,128)(2,1)}) %all-reduce.3.cloned.1.call-update) | async-done | bytes 4194320 | tf_op jit(solution)/shard_map/psum | solution.py:14
  222.9 2.9 convolution_convert_fusion
  225.8 0.0 all-to-all-done
  225.8 2.5 broadcast_in_dim.61
  228.3 70.1 %scatter_fusion = bf16[256,32,256]{2,1,0:T(8,128)(2,1)} fusion(bf16[256,32,256]{2,1,0:T(8,128)(2,1)} %broadcast_in_dim.61, s32[512]{0:T(512)S(1)} %bitcast.77, bf16[512,32,256]{2,1,0:T(8,128)(2,1)} %bitcast.10), kind=kCustom, calls=%fused_computation.1 | custom fusion | bytes 25167872 | tf_op jit(solution)/shard_map/scatter | solution.py:33
  298.5 6.9 %reshape.208 = bf16[16,512,1,2,128]{4,3,1,0,2:T(2,128)(2,1)} reshape(bf16[256,32,256]{2,1,0:T(8,128)(2,1)} %scatter_fusion) | data formatting | bytes 8388608 | tf_op jit(solution)/shard_map/reshape | solution.py:36
  305.4 3.8 copy_select_fusion
  309.2 0.0 copy-start.1
  309.2 1.9 copy-done.1
  311.1 0.6 fusion.9
  311.8 2.1 fusion.10
  313.8 5.4 %fusion = f32[16,8192]{1,0:T(8,128)} fusion(bf16[1,512,8192]{2,1,0:T(8,128)(2,1)} %param.14, bf16[2,8,4,128]{3,2,1,0:T(4,128)(2,1)S(1)} %bitcast.76), kind=kOutput, calls=%fused_computation.2 | convolution fusion | flops 134217728 | bytes 8929280 | tf_op jit(solution)/shard_map/dot_general | solution.py:60
  319.2 0.0 all-reduce.5.cloned.1.call-update
  319.2 64.2 %all-reduce.5.cloned.1.call-done = f32[16,8192]{1,0:T(8,128)} async-done(((f32[16,8192]{1,0:T(8,128)}), f32[16,8192]{1,0:T(8,128)}) %all-reduce.5.cloned.1.call-update) | async-done | bytes 524304 | tf_op jit(solution)/shard_map/psum | solution.py:61
  383.4 1.1 fusion.20
  384.5 1.3 collective-permute-start
  385.9 5.2 %broadcast_select_fusion = bf16[1,1,16,512,256]{4,3,2,1,0:T(8,128)(2,1)} fusion(bf16[1,1,16,512,256]{4,3,2,1,0:T(8,128)(2,1)} %bitcast.71, pred[16,512]{1,0:T(8,128)(4,1)S(1)} %get-tuple-element.3, bf16[16,256]{1,0:T(8,128)(2,1)S(1)} %convolution_convert_fusion), kind=kLoop, calls=%fused_computation.8 | loop fusion | flops 2097152 | bytes 8404992 | tf_op jit(solution)/shard_map/jit(_where)/select_n | solution.py:45
  391.1 2.4 collective-permute-done
  393.5 0.7 copy.28
  (5 shorter events, 0.0 us)
Async XLA Ops:
  29.8 196.0 %all-to-all-start = ((bf16[16,32,32,256]{3,2,1,0:T(8,128)(2,1)}), bf16[16,32,32,256]{3,2,1,0:T(8,128)(2,1)}, u32[]{:S(2)}, u32[]{:S(2)}) async-start(bf16[16,32,32,256]{3,2,1,0:T(8,128)(2,1)} %bitcast.72), calls=%async_computation | async-start | bytes 16777216 | tf_op jit(solution)/shard_map/all_to_all | solution.py:28
  38.5 184.4 %all-reduce.3.cloned.1.call-start = ((), (), s32[]{:S(2)}) async-start(), calls=%async_computation.1 | async-start | bytes 8388608 | tf_op jit(solution)/shard_map/psum | solution.py:14
  43.6 0.7 copy-start.3
  43.6 1.0 copy-start
  43.6 1.2 copy-start.2
  43.7 339.8 %all-reduce.5.cloned.1.call-start = ((), (), s32[]{:S(2)}) async-start(), calls=%async_computation.2 | async-start | bytes 1048576 | tf_op jit(solution)/shard_map/psum | solution.py:61
  44.8 4.7 %copy-start.4 = (s32[1,1,16]{2,1,0:T(1,128)S(1)}, s32[1,1,16]{2,1,0:T(1,128)}, u32[]{:S(2)}) copy-start(s32[1,1,16]{2,1,0:T(1,128)} %param.19) | copy-start | bytes 196
  309.2 1.9 copy-start.1
  384.5 8.9 %collective-permute-start = (bf16[16,8192]{1,0:T(8,128)(2,1)S(1)}, bf16[16,8192]{1,0:T(8,128)(2,1)S(1)}, u32[]{:S(2)}, u32[]{:S(2)}) collective-permute-start(bf16[16,8192]{1,0:T(8,128)(2,1)S(1)} %fusion.20), channel_id=1, source_target_pairs={{0,8},{8,16},{16,24},{24,32},{32,40},{40,48},{48,56},{56,0},{1,9},... | collective-permute-start | bytes 786440 | tf_op jit(solution)/shard_map/ppermute | solution.py:19
Sparse Core Ops, SparseCore 0:
  43.8 179.0 all-reduce.2
  319.4 64.0 all-reduce.4
where the time goes:
time: 406 us; the launch traced here: 401 us
  waiting for transfers between devices  240 us (59%)
  local copies, waits for them, and re-layouts  105 us (26%)
  other arithmetic  15.6 us (4%)
  matrix products  15.6 us (4%)
  between operations  14.8 us (4%)
  starting transfers between devices  10.3 us (3%)
    psum x1, waiting for transfers between devices, broadcast(): return lax.psum(kept, axis)  173 us
    scatter x1, local copies, waits for them, and re-layouts, shards(): moved.at[recv_slot[0].reshape(-1)]  70.1 us
    psum x1, waiting for transfers between devices, shards(): total = lax.psum(update, 'tp')  64.2 us
    gather x1, local copies, waits for them, and re-layouts, shards(): outgoing = old_pool[send_index[0]]  21.8 us
    select_n x2, other arithmetic, shards(): jnp.where(positions[None, :, None] == length[:, None, None], keyval[:, No...  9.03 us
    all_to_all x1, starting transfers between devices, shards(): lax.all_to_all(outgoing, ('rep', 'section'), split_axis=0, concat_axis=0,...  8.65 us
  transfers between devices with their start and end apart: 4, of which 3 were waited for; matrix products, arithmetic and copies ran while one was open for 4% of the time, Pallas kernels for 0%

commit v1 on v0

v1 whole, which is shorter than its diff:
```python
import functools

import jax
import jax.numpy as jnp
from jax import lax
from jax.experimental import pallas as pl
from jax.experimental.pallas import tpu as pltpu
from jax.sharding import PartitionSpec as P

HD = 128
CTX = 512
BLK = 32
MESH = pl.DeviceIdType.MESH
MIB = 2**20
FAR = (1, 3, 2)


def place():
    rep, section = lax.axis_index("rep"), lax.axis_index("section")
    return (section // 4) * 2 + rep, section % 4, lax.axis_index("tp")


def at(y, z):
    return {"rep": y % 2, "section": (y // 2) * 4 + z}


def group(y, z):
    return (y % 2) * 8 + (y // 2) * 4 + z


def remote(src, dst, send, recv, k, device):
    return pltpu.make_async_remote_copy(
        src_ref=src,
        dst_ref=dst,
        send_sem=send.at[k],
        recv_sem=recv.at[k],
        device_id=device,
        device_id_type=MESH,
    )


def move_kernel(
    sidx, holder, hidden, gain, pool_h, wq_h, wkv_h,
    land, q_o, kv_o,
    pool, stage, mid_a, mid_b, wq, wkv, hpeer, kvsend, kvpeer, normed,
    send, recv, side_send, side_recv, local,
):
    y, z, _ = place()
    rep = lax.axis_index("rep")
    half = stage.shape[1] // 2
    lo, hi = pl.ds(0, half), pl.ds(half, half)

    pool_in = pltpu.make_async_copy(pool_h, pool, local.at[0])
    pool_in.start()
    wkv_in = pltpu.make_async_copy(wkv_h, wkv, local.at[1])
    wq_in = pltpu.make_async_copy(wq_h, wq, local.at[2])

    barrier = pltpu.get_barrier_semaphore()
    for d in FAR:
        for device in (at((y + d) % 4, z), at(y, (z + d) % 4)):
            pl.semaphore_signal(barrier, inc=1, device_id=device, device_id_type=MESH)
    pl.semaphore_wait(barrier, 6)

    peer = {"rep": 1 - rep}
    to_peer = remote(hidden, hpeer, side_send, side_recv, 0, peer)
    to_peer.start()
    pool_in.wait()
    wkv_in.start()
    wq_in.start()

    def fill(dy, dz):
        g = group((y + dy) % 4, (z + dz) % 4)

        def body(i, _):
            for u in range(4):
                c = i * 4 + u
                stage[dy * 4 + dz, c] = pool[sidx[g, c]]
            return 0

        lax.fori_loop(0, stage.shape[1] // 4, body, 0)

    me = group(y, z)
    down, across = {}, {}
    for dz in FAR:
        for dy in FAR:
            fill(dy, dz)
            k = (dy - 1) * 3 + dz - 1
            src = stage.at[dy * 4 + dz]
            down[dy, dz] = remote(src.at[lo], mid_a.at[k], send, recv, k, at((y + dy) % 4, z))
            across[dy, dz] = remote(src.at[hi], mid_b.at[k], send, recv, 9 + k, at(y, (z + dz) % 4))
            down[dy, dz].start()
            across[dy, dz].start()
    last = []
    late = []
    for d in FAR:
        fill(d, 0)
        fill(0, d)
        along_y, along_z = stage.at[d * 4], stage.at[d]
        for first, src, part, k, device in (
            (True, along_y, lo, 18 + d - 1, at((y + d) % 4, z)),
            (True, along_z, hi, 21 + d - 1, at(y, (z + d) % 4)),
            (False, along_y, hi, 24 + d - 1, at((y + d) % 4, z)),
            (False, along_z, lo, 27 + d - 1, at(y, (z + d) % 4)),
        ):
            copy = remote(src.at[part], land.at[me, part], send, recv, k, device)
            (last if first else late).append(copy)
            if first:
                copy.start()
    fill(0, 0)
    keep = pltpu.make_async_copy(stage.at[0], land.at[me], local.at[3])
    keep.start()

    to_peer.wait_recv()
    width = hidden.shape[1]
    step = 1024
    rows = hidden.shape[0]

    def scale_of(ref):
        total = jnp.zeros((rows, 1), jnp.float32)
        for i in range(width // step):
            part = ref[:, i * step : (i + 1) * step].astype(jnp.float32)
            total = total + jnp.sum(part * part, axis=1, keepdims=True)
        return lax.rsqrt(total / width + 1e-05)

    own_scale, peer_scale = scale_of(hidden), scale_of(hpeer)
    for i in range(width // step):
        cut = slice(i * step, (i + 1) * step)
        g = gain[:, cut]
        normed[0:rows, cut] = (hidden[:, cut].astype(jnp.float32) * own_scale * g).astype(jnp.bfloat16)
        normed[rows : 2 * rows, cut] = (hpeer[:, cut].astype(jnp.float32) * peer_scale * g).astype(jnp.bfloat16)

    def product(count, weight):
        def body(i, total):
            cut = pl.ds(pl.multiple_of(i * step, step), step)
            return total + jnp.dot(normed[0:count, cut], weight[cut, :], preferred_element_type=jnp.float32)

        return lax.fori_loop(0, width // step, body, jnp.zeros((count, weight.shape[1]), jnp.float32))

    wkv_in.wait()
    both = product(2 * rows, wkv).astype(jnp.bfloat16)
    kvsend[...] = both[rows : 2 * rows]
    back = remote(kvsend, kvpeer, side_send, side_recv, 1, peer)
    back.start()
    wq_in.wait()
    query = product(rows, wq).astype(jnp.bfloat16).astype(jnp.float32)
    q_o[...] = jnp.zeros_like(q_o)
    for h in range(query.shape[1] // HD):
        q_o[:, h, :] = query[:, h * HD : (h + 1) * HD]

    for copy in late:
        copy.start()
    relays = []
    for dz in FAR:
        for dy in FAR:
            k = (dy - 1) * 3 + dz - 1
            down[dy, dz].wait_recv()
            source = group((y - dy + 4) % 4, z)
            relay = remote(mid_a.at[k], land.at[source, lo], send, recv, 30 + k, at(y, (z + dz) % 4))
            relay.start()
            relays.append(relay)
            across[dy, dz].wait_recv()
            source = group(y, (z - dz + 4) % 4)
            relay = remote(mid_b.at[k], land.at[source, hi], send, recv, 39 + k, at((y + dy) % 4, z))
            relay.start()
            relays.append(relay)

    back.wait_recv()
    mine = jnp.where(holder[0] == rep, jnp.float32(1), jnp.float32(0))
    own = both[0:rows].astype(jnp.float32)
    other = kvpeer[...].astype(jnp.float32)
    kv_o[...] = jnp.where(jnp.full(own.shape, mine) > 0.5, own, other).astype(jnp.bfloat16)

    for copy in last + late + relays:
        copy.wait_recv()
    for copy in [*down.values(), *across.values(), *last, *late, *relays, to_peer, back]:
        copy.wait_send()
    keep.wait()


def attend_kernel(inv, lengths, land, q, kv, w_h, cache, out, held, w, att, sems):
    w_in = pltpu.make_async_copy(w_h, w, sems.at[0])
    blocks = held.shape[0]

    def fetch(i, _):
        for u in range(8):
            j = i * 8 + u
            pltpu.make_async_copy(land.at[inv[j]], held.at[j], sems.at[1]).start()
        return 0

    lax.fori_loop(0, blocks // 8, fetch, 0)
    w_in.start()
    pltpu.make_async_copy(land.at[pl.ds(0, blocks)], held, sems.at[1]).wait()

    requests = q.shape[0]
    per = blocks // requests
    row = lax.broadcasted_iota(jnp.int32, held.shape[1:], 0)

    for b in range(requests):
        length = lengths[b]
        j = b * per + length // BLK
        held[j] = jnp.where(row == length % BLK, kv[b : b + 1, :].astype(jnp.float32), held[j].astype(jnp.float32)).astype(jnp.bfloat16)
    store = pltpu.make_async_copy(held, cache, sems.at[2])
    store.start()

    position = lax.broadcasted_iota(jnp.int32, (q.shape[1], CTX), 1)

    for b in range(requests):
        keys = held[b * per : (b + 1) * per, :, 0:HD].reshape(CTX, HD)
        values = held[b * per : (b + 1) * per, :, HD : 2 * HD].reshape(CTX, HD)
        scores = lax.dot_general(
            q[b].astype(jnp.bfloat16), keys, (((1,), (1,)), ((), ())), preferred_element_type=jnp.float32
        ) * HD ** (-0.5)
        valid = position <= lengths[b]
        expo = jnp.where(valid, jnp.exp(jnp.where(valid, scores, 0.0)), 0.0)
        weights = (expo / jnp.sum(expo, axis=1, keepdims=True)).astype(jnp.bfloat16)
        att[b] = jnp.dot(weights, values, preferred_element_type=jnp.float32)

    heads = w.shape[0] // HD
    attended = jnp.concatenate([att[:, h, :] for h in range(heads)], axis=1).astype(jnp.bfloat16)
    w_in.wait()
    step = 1024

    def body(i, _):
        cut = pl.ds(pl.multiple_of(i * step, step), step)
        out[:, cut] = jnp.dot(attended, w[:, cut], preferred_element_type=jnp.float32)
        return 0

    lax.fori_loop(0, w.shape[1] // step, body, 0)
    store.wait()


def sum_kernel(part, hidden, out, land, mine, send, recv):
    tp = lax.axis_index("tp")
    section = lax.axis_index("section")
    sections = lax.axis_size("section")
    count = lax.axis_size("tp")
    step = part.shape[1] // count

    def cut(t):
        return pl.ds(pl.multiple_of(t * step, step), step)

    barrier = pltpu.get_barrier_semaphore()
    for k in range(1, count):
        pl.semaphore_signal(barrier, inc=1, device_id={"tp": (tp + k) % count}, device_id_type=MESH)
    before = {"section": (section + sections - 1) % sections}
    pl.semaphore_signal(barrier, inc=1, device_id=before, device_id_type=MESH)
    pl.semaphore_wait(barrier, count)

    sums = []
    for k in range(1, count):
        t = (tp + k) % count
        copy = remote(part.at[:, cut(t)], land.at[k - 1], send, recv, k - 1, {"tp": t})
        copy.start()
        sums.append(copy)
    total = hidden[:, cut(tp)].astype(jnp.float32) + part[:, cut(tp)]
    for k in range(1, count):
        sums[k - 1].wait_recv()
        total = total + land[k - 1]
    mine[...] = total.astype(jnp.bfloat16)
    shift = remote(mine, out.at[:, cut(tp)], send, recv, count - 1, {"section": (section + 1) % sections})
    shift.start()
    shift.wait_recv()
    spread = []
    for k in range(1, count):
        copy = remote(out.at[:, cut(tp)], out.at[:, cut(tp)], send, recv, count + k - 1, {"tp": (tp + k) % count})
        copy.start()
        spread.append(copy)
    for copy in spread:
        copy.wait_recv()
    for copy in [*sums, shift, *spread]:
        copy.wait_send()


def shards(
    hidden, gain, w_query, w_keyval, w_out, old_pool, send_index, recv_slot, holder, lengths
):
    state = hidden[0, 0]
    requests, width = state.shape
    pool_blocks, blk, lanes = old_pool.shape
    groups, cap = send_index.shape[1:]
    blocks = requests * CTX // blk
    heads = w_query.shape[2] // HD
    vmem = pl.BlockSpec(memory_space=pltpu.VMEM)
    smem = pl.BlockSpec(memory_space=pltpu.SMEM)
    hbm = pl.BlockSpec(memory_space=pl.ANY)

    slots = recv_slot[0].reshape(1, -1)
    hit = slots == jnp.arange(blocks, dtype=jnp.int32)[:, None]
    inverse = jnp.sum(jnp.where(hit, jnp.arange(groups * cap, dtype=jnp.int32)[None, :], 0), axis=1)

    half = cap // 2
    land, query, keyval = pl.pallas_call(
        move_kernel,
        name="move",
        out_shape=(
            jax.ShapeDtypeStruct((groups, cap, blk, lanes), jnp.bfloat16),
            jax.ShapeDtypeStruct((requests, 8, HD), jnp.float32),
            jax.ShapeDtypeStruct((requests, lanes), jnp.bfloat16),
        ),
        in_specs=[smem, smem, vmem, vmem, hbm, hbm, hbm],
        out_specs=(hbm, vmem, vmem),
        scratch_shapes=[
            pltpu.VMEM((pool_blocks, blk, lanes), jnp.bfloat16),
            pltpu.VMEM((groups, cap, blk, lanes), jnp.bfloat16),
            pltpu.VMEM((9, half, blk, lanes), jnp.bfloat16),
            pltpu.VMEM((9, half, blk, lanes), jnp.bfloat16),
            pltpu.VMEM(w_query.shape[1:], jnp.bfloat16),
            pltpu.VMEM(w_keyval.shape[2:], jnp.bfloat16),
            pltpu.VMEM((requests, width), jnp.bfloat16),
            pltpu.VMEM((requests, lanes), jnp.bfloat16),
            pltpu.VMEM((requests, lanes), jnp.bfloat16),
            pltpu.VMEM((2 * requests, width), jnp.bfloat16),
            pltpu.SemaphoreType.DMA((48,)),
            pltpu.SemaphoreType.DMA((48,)),
            pltpu.SemaphoreType.DMA((2,)),
            pltpu.SemaphoreType.DMA((2,)),
            pltpu.SemaphoreType.DMA((4,)),
        ],
        compiler_params=pltpu.CompilerParams(
            collective_id=0, has_side_effects=True, vmem_limit_bytes=42 * MIB
        ),
    )(send_index[0], holder, state, gain, old_pool, w_query[0], w_keyval[0, 0])

    cache, part = pl.pallas_call(
        attend_kernel,
        name="attend",
        out_shape=(
            jax.ShapeDtypeStruct((blocks, blk, lanes), jnp.bfloat16),
            jax.ShapeDtypeStruct((requests, width), jnp.float32),
        ),
        in_specs=[smem, smem, hbm, vmem, vmem, hbm],
        out_specs=(hbm, vmem),
        scratch_shapes=[
            pltpu.VMEM((blocks, blk, lanes), jnp.bfloat16),
            pltpu.VMEM(w_out.shape[1:], jnp.bfloat16),
            pltpu.VMEM((requests, 8, HD), jnp.float32),
            pltpu.SemaphoreType.DMA((3,)),
        ],
        compiler_params=pltpu.CompilerParams(vmem_limit_bytes=24 * MIB),
    )(inverse, lengths[0, 0], land.reshape(groups * cap, blk, lanes), query, keyval, w_out[0])

    tp = lax.axis_size("tp")
    passed = pl.pallas_call(
        sum_kernel,
        name="sum",
        out_shape=jax.ShapeDtypeStruct((requests, width), jnp.bfloat16),
        in_specs=[vmem, vmem],
        out_specs=vmem,
        scratch_shapes=[
            pltpu.VMEM((tp - 1, requests, width // tp), jnp.float32),
            pltpu.VMEM((requests, width // tp), jnp.bfloat16),
            pltpu.SemaphoreType.DMA((2 * tp - 1,)),
            pltpu.SemaphoreType.DMA((2 * tp - 1,)),
        ],
        compiler_params=pltpu.CompilerParams(
            collective_id=1, has_side_effects=True, vmem_limit_bytes=8 * MIB
        ),
    )(part, state)
    return passed[None, None], cache.reshape(1, 1, requests, CTX, lanes)


def solution(mesh):
    in_specs = (
        P("rep", "section", None, None),
        P("section", None),
        P("section", None, "tp"),
        P("rep", "section", None, "tp"),
        P("section", "tp", None),
        P(("rep", "section"), None, "tp"),
        P(("rep", "section"), None, None),
        P(("rep", "section"), None, None),
        P("section"),
        P("rep", "section", None),
    )
    out_specs = (P("rep", "section", None, None), P("rep", "section", None, None, "tp"))
    return jax.shard_map(shards, mesh=mesh, in_specs=in_specs, out_specs=out_specs, check_vma=False)
```

time: 406 us -> 156 us (0.38); the launches traced: 401 us -> 155 us
  waiting for transfers between devices: 240 us -> 0 us
  Pallas kernels: 0 us -> 142 us
  local copies, waits for them, and re-layouts: 105 us -> 11.6 us
  matrix products: 15.6 us -> 0 us
  other arithmetic: 15.6 us -> 0.14 us
  between operations: 14.8 us -> 1.34 us
  starting transfers between devices: 10.3 us -> 0 us
    psum x2 -> x0, waiting for transfers between devices: 238 us -> none  [the longest x1 173 us: broadcast(): return lax.psum(kept, axis)]
    pallas_call x0 -> x3, Pallas kernels: none -> 142 us  [the longest x1 106 us: shards(): pl.pallas_call(move_kernel, name='move', out_shape=(jax.ShapeDtypeStruct(...]
    scatter x1 -> x0, local copies, waits for them, and re-layouts: 70.1 us -> none  [shards(): moved.at[recv_slot[0].reshape(-1)]]
    gather x1 -> x0, local copies, waits for them, and re-layouts: 21.8 us -> none  [shards(): outgoing = old_pool[send_index[0]]]
    dot_general x5 -> x0, matrix products: 15.6 us -> none  [the longest x1 5.39 us: shards(): update = jnp.dot(attended, w_out[0], preferred_element_type=jnp.float32)]
    select_n x5 -> x0, other arithmetic: 14.2 us -> none  [the longest x2 9.03 us: shards(): jnp.where(positions[None, :, None] == length[:, None, None], keyval[:, No...]
    all_to_all x1 -> x0, starting transfers between devices: 8.65 us -> none  [shards(): lax.all_to_all(outgoing, ('rep', 'section'), split_axis=0, concat_axis=0,...]
    unnamed x11 -> x17, local copies, waits for them, and re-layouts: 3.27 us -> 10.9 us
  transfers between devices with their start and end apart: 4 -> 0, of which waited for: 3 -> 0; matrix products, arithmetic and copies ran while one was open for 4% -> 0% of each run, Pallas kernels for 0% -> 0%
where the time goes in v1:
time: 156 us; the launch traced here: 155 us
  Pallas kernels  142 us (91%)
  local copies, waits for them, and re-layouts  11.6 us (7%)
    pallas_call x1, Pallas kernels, shards(): pl.pallas_call(move_kernel, name='move', out_shape=(jax.ShapeDtypeStruct(...  106 us
    pallas_call x1, Pallas kernels, shards(): pl.pallas_call(sum_kernel, name='sum', out_shape=jax.ShapeDtypeStruct((re...  22.5 us
    pallas_call x1, Pallas kernels, shards(): pl.pallas_call(attend_kernel, name='attend', out_shape=(jax.ShapeDtypeStr...  13.9 us
    unnamed x17, local copies, waits for them, and re-layouts  10.9 us

profile of v1, /device:TPU:1, one launch (start us, length us, event | category | flops | bytes accessed | tf_op | source)
XLA Modules:
  0.0 155.2 jit_solution(3377665709475375642)
XLA Ops:
  1.3 0.8 eq.15
  2.1 0.1 select_reduce_fusion.inv
  2.2 0.0 copy-start.2
  2.2 2.2 %copy-done.2 = bf16[256,32,256]{2,1,0:T(8,128)(2,1)S(1)} copy-done((bf16[256,32,256]{2,1,0:T(8,128)(2,1)S(1)}, bf16[256,32,256]{2,1,0:T(8,128)(2,1)}, u32[]{:S(2)}) %copy-start.2) | copy-done | bytes 4194328
  4.4 0.0 copy-start.3
  4.4 2.2 %copy-done.3 = bf16[1,1,8192,256]{3,2,1,0:T(8,128)(2,1)S(1)} copy-done((bf16[1,1,8192,256]{3,2,1,0:T(8,128)(2,1)S(1)}, bf16[1,1,8192,256]{3,2,1,0:T(8,128)(2,1)}, u32[]{:S(2)}) %copy-start.3) | copy-done | bytes 4194328
  6.6 0.0 copy-start.4
  6.6 0.9 copy-done.4
  7.5 0.0 copy-start.5
  7.5 0.8 copy-done.5
  8.3 0.0 copy-start.6
  8.3 0.7 copy-done.6
  9.0 0.0 copy-start
  9.0 0.0 copy-start.7
  9.0 105.6 %move.1 = (bf16[16,32,32,256]{3,2,1,0:T(8,128)(2,1)}, f32[16,8,128]{2,1,0:T(8,128)S(1)}, bf16[16,256]{1,0:T(8,128)(2,1)S(1)}) custom-call(s32[16,32]{1,0:T(8,128)S(1)} %bitcast.15, s32[1]{0:T(128)S(6)} %copy.13.holder, bf16[16,8192]{1,0:T(8,128)(2,1)S(1)} %bitcast.12, f32[1,8192]{1,0:T(1,128)S(1)} %copy-done.5, bf16[256,32,256]{2,1,0:T(8,128)(2,1)S(1)} %copy-done.2, ...), custom_call_target="tpu_custom_call" | custom-call | tf_op jit(solution)/shard_map/move/pallas_call | solution.py:292
  114.6 0.0 copy-done
  114.6 0.0 copy-done.7
  114.6 0.0 copy-start.1
  114.7 3.4 %copy-done.1 = bf16[16,32,32,256]{3,2,1,0:T(8,128)(2,1)S(1)} copy-done((bf16[16,32,32,256]{3,2,1,0:T(8,128)(2,1)S(1)}, bf16[16,32,32,256]{3,2,1,0:T(8,128)(2,1)}, u32[]{:S(2)}) %copy-start.1) | copy-done | bytes 8388632
  118.0 13.9 %attend.1 = (bf16[256,32,256]{2,1,0:T(8,128)(2,1)}, f32[16,8192]{1,0:T(8,128)S(1)}) custom-call(s32[256]{0:T(256)S(1)} %select_reduce_fusion.inv, s32[16]{0:T(128)S(1)} %bitcast.16, bf16[512,32,256]{2,1,0:T(8,128)(2,1)S(1)} %bitcast.10, f32[16,8,128]{2,1,0:T(8,128)S(1)} %get-tuple-element.8.q, bf16[16,256]{1,0:T(8,128)(2,1)S(1)} %get-tuple-element.9.kv, ...), custom_call_target="tpu_custom_call" | custom-call | tf_op jit(solution)/shard_map/attend/pallas_call | solution.py:324
  132.0 22.5 %sum.1 = bf16[16,8192]{1,0:T(8,128)(2,1)S(1)} custom-call(f32[16,8192]{1,0:T(8,128)S(1)} %get-tuple-element.10.part, bf16[16,8192]{1,0:T(8,128)(2,1)S(1)} %bitcast.13), custom_call_target="tpu_custom_call" | custom-call | tf_op jit(solution)/shard_map/sum/pallas_call | solution.py:343
  154.5 0.7 copy.14
Async XLA Ops:
  2.2 2.2 %copy-start.2 = (bf16[256,32,256]{2,1,0:T(8,128)(2,1)S(1)}, bf16[256,32,256]{2,1,0:T(8,128)(2,1)}, u32[]{:S(2)}) copy-start(bf16[256,32,256]{2,1,0:T(8,128)(2,1)} %pool_h.1) | copy-start | bytes 12582916
  4.4 2.2 %copy-start.3 = (bf16[1,1,8192,256]{3,2,1,0:T(8,128)(2,1)S(1)}, bf16[1,1,8192,256]{3,2,1,0:T(8,128)(2,1)}, u32[]{:S(2)}) copy-start(bf16[1,1,8192,256]{3,2,1,0:T(8,128)(2,1)} %param.13) | copy-start | bytes 12582916
  6.6 0.9 copy-start.4
  7.5 0.8 copy-start.5
  8.3 0.7 copy-start.6
  9.0 105.7 %copy-start = (bf16[1,512,8192]{2,1,0:T(8,128)(2,1)S(1)}, bf16[1,512,8192]{2,1,0:T(8,128)(2,1)}, u32[]{:S(2)}) copy-start(bf16[1,512,8192]{2,1,0:T(8,128)(2,1)} %param.14) | copy-start | bytes 25165828
  9.0 105.7 %copy-start.7 = (s32[1,1,16]{2,1,0:T(1,128)S(1)}, s32[1,1,16]{2,1,0:T(1,128)}, u32[]{:S(2)}) copy-start(s32[1,1,16]{2,1,0:T(1,128)} %param.19) | copy-start | bytes 196
  114.6 3.4 %copy-start.1 = (bf16[16,32,32,256]{3,2,1,0:T(8,128)(2,1)S(1)}, bf16[16,32,32,256]{3,2,1,0:T(8,128)(2,1)}, u32[]{:S(2)}) copy-start(bf16[16,32,32,256]{3,2,1,0:T(8,128)(2,1)} %get-tuple-element.7) | copy-start | bytes 25165828

commit v2 on v1

--- a/solution.py
+++ b/solution.py
@@ -13,6 +13,10 @@
 MESH = pl.DeviceIdType.MESH
 MIB = 2**20
 FAR = (1, 3, 2)
+CAP_ONE = 42
+CAP_TWO = 42
+STAY = 128
+BALANCE = 0.01
 
 
 def place():
@@ -39,77 +43,291 @@
     )
 
 
+def dot(a, b):
+    return jnp.dot(a.astype(jnp.bfloat16), b.astype(jnp.bfloat16), preferred_element_type=jnp.float32)
+
+
+def dot_t(a, b):
+    return lax.dot_general(
+        a.astype(jnp.bfloat16), b.astype(jnp.bfloat16), (((1,), (1,)), ((), ())), preferred_element_type=jnp.float32
+    )
+
+
+def grid(rows, columns):
+    return (
+        lax.broadcasted_iota(jnp.int32, (rows, columns), 0),
+        lax.broadcasted_iota(jnp.int32, (rows, columns), 1),
+    )
+
+
+def ones(condition):
+    return jnp.where(condition, 1.0, 0.0).astype(jnp.float32)
+
+
+def ring_order(table):
+    return jnp.concatenate([table[0:4], table[8:12], table[4:8], table[12:16]], axis=0).astype(jnp.float32)
+
+
+def widen(table):
+    k, lane = grid(32, 128)
+    return dot(table, ones(k == lane % 32))
+
+
+def pack_y(table):
+    row, lane = grid(16, 128)
+    r, k = grid(8, 16)
+    return dot(ones(k // 4 == r), jnp.where(lane // 32 == row % 4, table, 0.0))
+
+
+def pack_z(table):
+    row, lane = grid(16, 128)
+    r, k = grid(8, 16)
+    return dot(ones((k % 4 == r) & (r < 4)), jnp.where(lane // 32 == row // 4, table, 0.0))
+
+
+def ranks(valid):
+    k, lane = grid(128, 128)
+    return dot(valid, ones((k < lane) & (k // 32 == lane // 32)))
+
+
+def route(masks, y, z):
+    flat = masks[...].reshape(128, 128)
+    k, lane = grid(128, 128)
+    per = dot(flat, ones((k // 32 == lane % 4) & (lane < 16)))
+    per = jnp.where((lane // 4 == k % 8) & (lane < 16), per, 0.0)
+    g, k = grid(16, 128)
+    counts = dot(ones(k // 8 == (g % 4) * 4 + g // 4), per)
+
+    g, h = grid(16, 128)
+    inside = h < 16
+    off_y = ones((g // 4 != h // 4) & inside)
+    off_z = ones((g % 4 != h % 4) & inside)
+    a, b = grid(16, 16)
+    same_y, same_z = ones(a // 4 == b // 4), ones(a % 4 == b % 4)
+    a, b = grid(128, 128)
+    both = (a < 16) & (b < 16)
+    along_y, along_z = ones((a // 4 == b // 4) & both), ones((a % 4 == b % 4) & both)
+
+    def loads(first, second):
+        return (
+            dot(same_y, first) * off_y,
+            dot(same_z, second) * off_z,
+            dot(first, along_z) * off_z,
+            dot(second, along_y) * off_y,
+        )
+
+    share = jnp.full((16, 128), 0.5, jnp.float32)
+    for _ in range(4):
+        a1, b1, a2, b2 = loads(counts * share, counts - counts * share)
+        share = jnp.clip(share + BALANCE * (jnp.maximum(b1, b2) - jnp.maximum(a1, a2)), 0.0, 1.0)
+    share = jnp.where(g == h, 1.0, share)
+    first = jnp.floor(counts * share + 0.5)
+    second = counts - first
+    a1, b1, a2, b2 = loads(first, second)
+    over = jnp.maximum(jnp.maximum(a1, b1) - CAP_ONE, jnp.maximum(a2, b2) - CAP_TWO)
+    return first, second, jnp.max(over, keepdims=True)
+
+
+def offsets(first, second):
+    a, b = grid(16, 16)
+    one_first = dot(ones((a // 4 == b // 4) & (b % 4 < a % 4)), first)
+    one_second = dot(ones((a % 4 == b % 4) & (b // 4 < a // 4)), second)
+    a, b = grid(128, 128)
+    both = (a < 16) & (b < 16)
+    two_first = dot(first, ones((a % 4 == b % 4) & (a // 4 < b // 4) & both))
+    two_second = dot(second, ones((a // 4 == b // 4) & (a % 4 < b % 4) & both))
+    return one_first, one_second, two_first, two_second
+
+
+def first_tables(masks, index, first, one_first, one_second, y, z, blocks_held):
+    flat = masks[...].reshape(128, 128)
+    g, k = grid(16, 128)
+    mine = dot(ones(k == ((g % 4) * 4 + g // 4) * 8 + y), flat)
+    k, lane = grid(128, 128)
+    mine = dot(mine, ones(k == z * 32 + lane % 32))
+    g, h = grid(16, 128)
+
+    def column(table):
+        picked = jnp.sum(jnp.where(h == y * 4 + z, table, 0.0), axis=1, keepdims=True)
+        return jnp.broadcast_to(picked, (16, 128))
+
+    taken = column(first)
+    place, lane = grid(128, 128)
+    row, _ = grid(8, 128)
+    out = []
+    for pack, start, is_first in ((pack_y, one_first, True), (pack_z, one_second, False)):
+        valid = pack(mine)
+        rank = ranks(valid)
+        limit = pack(taken)
+        begin = pack(column(start))
+        blocks = pack(index)
+        if is_first:
+            keep, at_place = (valid > 0.5) & (rank < limit), begin + rank
+        else:
+            keep, at_place = (valid > 0.5) & (rank >= limit), begin + rank - limit
+        at_place = jnp.where(keep, at_place, -1.0)
+        table = jnp.zeros((8, 128), jnp.float32)
+        for m in range(4):
+            hit = ones(at_place[m : m + 1, :].astype(jnp.int32) == place)
+            table = jnp.where(row == m, dot_t(blocks, hit), table)
+        out.append(table)
+    return jnp.clip(jnp.concatenate(out, axis=0).astype(jnp.int32), 0, blocks_held - 1)
+
+
+def second_tables(first, second, one_first, one_second, two_first, two_second, y, z):
+    r, k = grid(8, 16)
+    row, lane = grid(8, 128)
+    spot = lane.astype(jnp.float32)
+    last = STAY + 3 * CAP_ONE - 1
+    out = []
+    for count, one, two, rows, me, far in (
+        (first, one_first, two_first, ones((k == y * 4 + r) & (r < 4)), y, lambda i: i * 4 + z),
+        (second, one_second, two_second, ones((k == r * 4 + z) & (r < 4)), z, lambda i: y * 4 + i),
+    ):
+        count, one, two = dot(rows, count), dot(rows, one), dot(rows, two)
+        table = jnp.zeros((8, 128), jnp.float32)
+        for i in range(4):
+            pick = lane == far(i)
+            n = jnp.sum(jnp.where(pick, count, 0.0), axis=1, keepdims=True)
+            begin = jnp.sum(jnp.where(pick, one, 0.0), axis=1, keepdims=True)
+            shift = jnp.sum(jnp.where(pick, two, 0.0), axis=1, keepdims=True)
+            base = part_of((me - i + 4) % 4, CAP_ONE)
+            inside = (spot >= shift) & (spot < shift + n)
+            table = jnp.where(inside, begin + spot - shift + jnp.full((8, 128), base).astype(jnp.float32), table)
+        out.append(table)
+    return jnp.clip(jnp.concatenate(out, axis=0).astype(jnp.int32), 0, last)
+
+
+def part_of(distance, cap):
+    return jnp.where(distance == 0, 0, STAY + (distance - 1) * cap)
+
+
+def final_table(slots, first, two_first, two_second, y, z):
+    valid = ones(slots < 255.5)
+    rank = ranks(valid)
+    r, k = grid(8, 16)
+    row, lane = grid(8, 128)
+    a, b = grid(128, 128)
+    spread = ones((a % 4 == b // 32) & (a < 16))
+
+    def own(table):
+        picked = dot(ones(k == y * 4 + z), table)
+        return dot(jnp.where((lane // 4 == row) & (lane < 16), picked, 0.0), spread)
+
+    limit, shift_first, shift_second = own(first), own(two_first), own(two_second)
+    total = STAY + 3 * CAP_TWO
+    base_first = part_of((z - lane // 32 + 4) % 4, CAP_TWO).astype(jnp.float32)
+    base_second = (part_of((y - row + 8) % 4, CAP_TWO) + total).astype(jnp.float32)
+    spot = jnp.where(rank < limit, base_first + shift_first + rank, base_second + shift_second + rank - limit)
+    spot = jnp.clip(spot, 0.0, float(2 * total - 1))
+    high = jnp.floor(spot / 16.0)
+    low = spot - high * 16.0
+    place, _ = grid(256, 128)
+    found = jnp.zeros((8, 256), jnp.float32)
+    for m in range(4):
+        hit = ones(slots[m : m + 1, :].astype(jnp.int32) == place)
+        found = found + dot_t(jnp.where(row == m, high, 0.0), hit) * 16.0 + dot_t(jnp.where(row == m, low, 0.0), hit)
+    return jnp.clip(jnp.sum(found, axis=0, keepdims=True).astype(jnp.int32), 0, 2 * total - 1)
+
+
 def move_kernel(
-    sidx, holder, hidden, gain, pool_h, wq_h, wkv_h,
-    land, q_o, kv_o,
-    pool, stage, mid_a, mid_b, wq, wkv, hpeer, kvsend, kvpeer, normed,
-    send, recv, side_send, side_recv, local,
+    recv_h, sidx_h, holder, hidden_h, gain_h, pool_h, wq_h, wkv_h,
+    fin, q_o, kv_o, inv_o, over_o,
+    recv_v, sidx_v, pool, masks, one_v, two_v, one_s, two_s, stage_one, mid, stage_two, wq, wkv, hidden, gain, hpeer,
+    kvsend, kvpeer, normed,
+    send, recv, side_send, side_recv, mask_send, mask_recv, local,
 ):
     y, z, _ = place()
     rep = lax.axis_index("rep")
-    half = stage.shape[1] // 2
-    lo, hi = pl.ds(0, half), pl.ds(half, half)
-
-    pool_in = pltpu.make_async_copy(pool_h, pool, local.at[0])
-    pool_in.start()
-    wkv_in = pltpu.make_async_copy(wkv_h, wkv, local.at[1])
-    wq_in = pltpu.make_async_copy(wq_h, wq, local.at[2])
+    copies = [
+        pltpu.make_async_copy(src, dst, local.at[i])
+        for i, (src, dst) in enumerate(
+            ((recv_h, recv_v), (sidx_h, sidx_v), (hidden_h, hidden), (pool_h, pool), (gain_h, gain), (wkv_h, wkv), (wq_h, wq))
+        )
+    ]
+    recv_in, sidx_in, hidden_in, pool_in, gain_in, wkv_in, wq_in = copies
+    for copy in copies[:5]:
+        copy.start()
 
     barrier = pltpu.get_barrier_semaphore()
     for d in FAR:
         for device in (at((y + d) % 4, z), at(y, (z + d) % 4)):
             pl.semaphore_signal(barrier, inc=1, device_id=device, device_id_type=MESH)
+
+    recv_in.wait()
+    row, _ = grid(8, 128)
+    slots = jnp.where(row < 4, pack_y(widen(ring_order(recv_v[...]))), 256.0)
+    masks[z, y] = ones(slots < 255.5)
     pl.semaphore_wait(barrier, 6)
 
+    hops = []
+    for d in FAR:
+        copy = remote(masks.at[z, y], masks.at[z, y], mask_send, mask_recv, d - 1, at((y + d) % 4, z))
+        copy.start()
+        hops.append(copy)
+    for copy in hops:
+        copy.wait_recv()
+    for d in FAR:
+        copy = remote(masks.at[z], masks.at[z], mask_send, mask_recv, 3 + d - 1, at(y, (z + d) % 4))
+        copy.start()
+        hops.append(copy)
+    for copy in hops[3:]:
+        copy.wait_recv()
+    for copy in hops:
+        copy.wait_send()
+
     peer = {"rep": 1 - rep}
+    hidden_in.wait()
     to_peer = remote(hidden, hpeer, side_send, side_recv, 0, peer)
     to_peer.start()
+
+    first, second, over = route(masks, y, z)
+    one_first, one_second, two_first, two_second = offsets(first, second)
+    sidx_in.wait()
+    index = widen(ring_order(sidx_v[...]))
+    one_v[...] = first_tables(masks, index, first, one_first, one_second, y, z, pool.shape[0])
+    one_in = pltpu.make_async_copy(one_v, one_s, local.at[7])
+    one_in.start()
+    over_o[...] = jnp.broadcast_to(over, over_o.shape).astype(jnp.int32)
     pool_in.wait()
+    one_in.wait()
+
+    def pack(dst, begin, count, src, table, line):
+        unroll = 8 if count % 8 == 0 else 6
+
+        def body(i, _):
+            for u in range(unroll):
+                p = i * unroll + u
+                dst[begin + p] = src[table[line, p]]
+            return 0
+
+        lax.fori_loop(0, count // unroll, body, 0)
+
+    stay_one = STAY + 3 * CAP_ONE
+    stay_two = STAY + 3 * CAP_TWO
+    started = []
+    for d in FAR:
+        for way, line, device in ((0, (y + d) % 4, at((y + d) % 4, z)), (1, 8 + (z + d) % 4, at(y, (z + d) % 4))):
+            begin = (way * 3 + d - 1) * CAP_ONE
+            pack(stage_one, begin, CAP_ONE, pool, one_s, line)
+            copy = remote(
+                stage_one.at[pl.ds(begin, CAP_ONE)],
+                mid.at[way, pl.ds(STAY + (d - 1) * CAP_ONE, CAP_ONE)],
+                send, recv, way * 3 + d - 1, device,
+            )
+            copy.start()
+            started.append(copy)
     wkv_in.start()
     wq_in.start()
-
-    def fill(dy, dz):
-        g = group((y + dy) % 4, (z + dz) % 4)
-
-        def body(i, _):
-            for u in range(4):
-                c = i * 4 + u
-                stage[dy * 4 + dz, c] = pool[sidx[g, c]]
-            return 0
-
-        lax.fori_loop(0, stage.shape[1] // 4, body, 0)
-
-    me = group(y, z)
-    down, across = {}, {}
-    for dz in FAR:
-        for dy in FAR:
-            fill(dy, dz)
-            k = (dy - 1) * 3 + dz - 1
-            src = stage.at[dy * 4 + dz]
-            down[dy, dz] = remote(src.at[lo], mid_a.at[k], send, recv, k, at((y + dy) % 4, z))
-            across[dy, dz] = remote(src.at[hi], mid_b.at[k], send, recv, 9 + k, at(y, (z + dz) % 4))
-            down[dy, dz].start()
-            across[dy, dz].start()
-    last = []
-    late = []
-    for d in FAR:
-        fill(d, 0)
-        fill(0, d)
-        along_y, along_z = stage.at[d * 4], stage.at[d]
-        for first, src, part, k, device in (
-            (True, along_y, lo, 18 + d - 1, at((y + d) % 4, z)),
-            (True, along_z, hi, 21 + d - 1, at(y, (z + d) % 4)),
-            (False, along_y, hi, 24 + d - 1, at((y + d) % 4, z)),
-            (False, along_z, lo, 27 + d - 1, at(y, (z + d) % 4)),
-        ):
-            copy = remote(src.at[part], land.at[me, part], send, recv, k, device)
-            (last if first else late).append(copy)
-            if first:
-                copy.start()
-    fill(0, 0)
-    keep = pltpu.make_async_copy(stage.at[0], land.at[me], local.at[3])
-    keep.start()
-
+    pack(mid.at[0], 0, STAY, pool, one_s, y)
+    pack(mid.at[1], 0, STAY, pool, one_s, 8 + z)
+
+    two_v[...] = second_tables(first, second, one_first, one_second, two_first, two_second, y, z)
+    two_in = pltpu.make_async_copy(two_v, two_s, local.at[8])
+    two_in.start()
+    inv_o[...] = final_table(slots, first, two_first, two_second, y, z)
+
+    gain_in.wait()
     to_peer.wait_recv()
     width = hidden.shape[1]
     step = 1024
@@ -146,35 +364,74 @@
     q_o[...] = jnp.zeros_like(q_o)
     for h in range(query.shape[1] // HD):
         q_o[:, h, :] = query[:, h * HD : (h + 1) * HD]
-
-    for copy in late:
-        copy.start()
-    relays = []
-    for dz in FAR:
-        for dy in FAR:
-            k = (dy - 1) * 3 + dz - 1
-            down[dy, dz].wait_recv()
-            source = group((y - dy + 4) % 4, z)
-            relay = remote(mid_a.at[k], land.at[source, lo], send, recv, 30 + k, at(y, (z + dz) % 4))
-            relay.start()
-            relays.append(relay)
-            across[dy, dz].wait_recv()
-            source = group(y, (z - dz + 4) % 4)
-            relay = remote(mid_b.at[k], land.at[source, hi], send, recv, 39 + k, at((y + dy) % 4, z))
-            relay.start()
-            relays.append(relay)
-
     back.wait_recv()
     mine = jnp.where(holder[0] == rep, jnp.float32(1), jnp.float32(0))
     own = both[0:rows].astype(jnp.float32)
     other = kvpeer[...].astype(jnp.float32)
     kv_o[...] = jnp.where(jnp.full(own.shape, mine) > 0.5, own, other).astype(jnp.bfloat16)
 
-    for copy in last + late + relays:
+    two_in.wait()
+    for copy in started:
         copy.wait_recv()
-    for copy in [*down.values(), *across.values(), *last, *late, *relays, to_peer, back]:
+    relays = []
+    for d in FAR:
+        for way, line, device in ((0, (z + d) % 4, at(y, (z + d) % 4)), (1, 8 + (y + d) % 4, at((y + d) % 4, z))):
+            begin = STAY + (d - 1) * CAP_TWO
+            pack(stage_two.at[way], begin, CAP_TWO, mid.at[way], two_s, line)
+            copy = remote(
+                stage_two.at[way, pl.ds(begin, CAP_TWO)],
+                fin.at[pl.ds(way * stay_two + begin, CAP_TWO)],
+                send, recv, 6 + way * 3 + d - 1, device,
+            )
+            copy.start()
+            relays.append(copy)
+    keep = []
+    for way, line in ((0, z), (1, 8 + y)):
+        pack(stage_two.at[way], 0, STAY, mid.at[way], two_s, line)
+        copy = pltpu.make_async_copy(
+            stage_two.at[way, pl.ds(0, STAY)], fin.at[pl.ds(way * stay_two, STAY)], local.at[9 + way]
+        )
+        copy.start()
+        keep.append(copy)
+    for copy in [to_peer, back, *started]:
         copy.wait_send()
-    keep.wait()
+    for copy in relays:
+        copy.wait_recv()
+    for copy in relays:
+        copy.wait_send()
+    for copy in keep:
+        copy.wait()
+
+
+def whole_kernel(sidx, pool_h, land, pool, stage, send, recv, local):
+    y, z, _ = place()
+    pool_in = pltpu.make_async_copy(pool_h, pool, local.at[0])
+    pool_in.start()
+    pairs = [(dy, dz) for dy in range(4) for dz in range(4) if dy or dz]
+    barrier = pltpu.get_barrier_semaphore()
+    for dy, dz in pairs:
+        pl.semaphore_signal(barrier, inc=1, device_id=at((y + dy) % 4, (z + dz) % 4), device_id_type=MESH)
+    pl.semaphore_wait(barrier, len(pairs))
+    pool_in.wait()
+    me = group(y, z)
+    copies = []
+    for dy, dz in [(0, 0), *pairs]:
+        g = group((y + dy) % 4, (z + dz) % 4)
+        k = dy * 4 + dz
+
+        def body(c, _):
+            stage[k, c] = pool[sidx[g, c]]
+            return 0
+
+        lax.fori_loop(0, stage.shape[1], body, 0)
+        if k:
+            copy = remote(stage.at[k], land.at[me], send, recv, k - 1, at((y + dy) % 4, (z + dz) % 4))
+        else:
+            copy = pltpu.make_async_copy(stage.at[0], land.at[me], local.at[1])
+        copy.start()
+        copies.append(copy)
+    for copy in copies:
+        copy.wait()
 
 
 def attend_kernel(inv, lengths, land, q, kv, w_h, cache, out, held, w, att, sems):
@@ -284,60 +541,98 @@
     smem = pl.BlockSpec(memory_space=pltpu.SMEM)
     hbm = pl.BlockSpec(memory_space=pl.ANY)
 
-    slots = recv_slot[0].reshape(1, -1)
-    hit = slots == jnp.arange(blocks, dtype=jnp.int32)[:, None]
-    inverse = jnp.sum(jnp.where(hit, jnp.arange(groups * cap, dtype=jnp.int32)[None, :], 0), axis=1)
-
-    half = cap // 2
-    land, query, keyval = pl.pallas_call(
+    places = 2 * (STAY + 3 * CAP_TWO)
+    dma = pltpu.SemaphoreType.DMA
+    land, query, keyval, table, over = pl.pallas_call(
         move_kernel,
         name="move",
         out_shape=(
-            jax.ShapeDtypeStruct((groups, cap, blk, lanes), jnp.bfloat16),
+            jax.ShapeDtypeStruct((places, blk, lanes), jnp.bfloat16),
             jax.ShapeDtypeStruct((requests, 8, HD), jnp.float32),
             jax.ShapeDtypeStruct((requests, lanes), jnp.bfloat16),
+            jax.ShapeDtypeStruct((1, blocks), jnp.int32),
+            jax.ShapeDtypeStruct((8, 128), jnp.int32),
         ),
-        in_specs=[smem, smem, vmem, vmem, hbm, hbm, hbm],
-        out_specs=(hbm, vmem, vmem),
+        in_specs=[hbm, hbm, smem, hbm, hbm, hbm, hbm, hbm],
+        out_specs=(hbm, vmem, vmem, vmem, vmem),
         scratch_shapes=[
+            pltpu.VMEM((groups, cap), jnp.int32),
+            pltpu.VMEM((groups, cap), jnp.int32),
             pltpu.VMEM((pool_blocks, blk, lanes), jnp.bfloat16),
-            pltpu.VMEM((groups, cap, blk, lanes), jnp.bfloat16),
-            pltpu.VMEM((9, half, blk, lanes), jnp.bfloat16),
-            pltpu.VMEM((9, half, blk, lanes), jnp.bfloat16),
+            pltpu.VMEM((4, 4, 8, 128), jnp.float32),
+            pltpu.VMEM((16, 128), jnp.int32),
+            pltpu.VMEM((16, 128), jnp.int32),
+            pltpu.SMEM((16, 128), jnp.int32),
+            pltpu.SMEM((16, 128), jnp.int32),
+            pltpu.VMEM((6 * CAP_ONE, blk, lanes), jnp.bfloat16),
+            pltpu.VMEM((2, STAY + 3 * CAP_ONE, blk, lanes), jnp.bfloat16),
+            pltpu.VMEM((2, STAY + 3 * CAP_TWO, blk, lanes), jnp.bfloat16),
             pltpu.VMEM(w_query.shape[1:], jnp.bfloat16),
             pltpu.VMEM(w_keyval.shape[2:], jnp.bfloat16),
+            pltpu.VMEM((requests, width), jnp.bfloat16),
+            pltpu.VMEM((1, width), jnp.float32),
             pltpu.VMEM((requests, width), jnp.bfloat16),
             pltpu.VMEM((requests, lanes), jnp.bfloat16),
             pltpu.VMEM((requests, lanes), jnp.bfloat16),
             pltpu.VMEM((2 * requests, width), jnp.bfloat16),
-            pltpu.SemaphoreType.DMA((48,)),
-            pltpu.SemaphoreType.DMA((48,)),
-            pltpu.SemaphoreType.DMA((2,)),
-            pltpu.SemaphoreType.DMA((2,)),
-            pltpu.SemaphoreType.DMA((4,)),
+            dma((12,)),
+            dma((12,)),
+            dma((2,)),
+            dma((2,)),
+            dma((6,)),
+            dma((6,)),
+            dma((11,)),
         ],
         compiler_params=pltpu.CompilerParams(
-            collective_id=0, has_side_effects=True, vmem_limit_bytes=42 * MIB
+            collective_id=0, has_side_effects=True, vmem_limit_bytes=60 * MIB
         ),
-    )(send_index[0], holder, state, gain, old_pool, w_query[0], w_keyval[0, 0])
-
-    cache, part = pl.pallas_call(
-        attend_kernel,
-        name="attend",
-        out_shape=(
-            jax.ShapeDtypeStruct((blocks, blk, lanes), jnp.bfloat16),
-            jax.ShapeDtypeStruct((requests, width), jnp.float32),
-        ),
-        in_specs=[smem, smem, hbm, vmem, vmem, hbm],
-        out_specs=(hbm, vmem),
-        scratch_shapes=[
-            pltpu.VMEM((blocks, blk, lanes), jnp.bfloat16),
-            pltpu.VMEM(w_out.shape[1:], jnp.bfloat16),
-            pltpu.VMEM((requests, 8, HD), jnp.float32),
-            pltpu.SemaphoreType.DMA((3,)),
-        ],
-        compiler_params=pltpu.CompilerParams(vmem_limit_bytes=24 * MIB),
-    )(inverse, lengths[0, 0], land.reshape(groups * cap, blk, lanes), query, keyval, w_out[0])
+    )(recv_slot[0], send_index[0], holder, state, gain, old_pool, w_query[0], w_keyval[0, 0])
+
+    def attend(inverse, held):
+        return pl.pallas_call(
+            attend_kernel,
+            name="attend",
+            out_shape=(
+                jax.ShapeDtypeStruct((blocks, blk, lanes), jnp.bfloat16),
+                jax.ShapeDtypeStruct((requests, width), jnp.float32),
+            ),
+            in_specs=[smem, smem, hbm, vmem, vmem, hbm],
+            out_specs=(hbm, vmem),
+            scratch_shapes=[
+                pltpu.VMEM((blocks, blk, lanes), jnp.bfloat16),
+                pltpu.VMEM(w_out.shape[1:], jnp.bfloat16),
+                pltpu.VMEM((requests, 8, HD), jnp.float32),
+                dma((3,)),
+            ],
+            compiler_params=pltpu.CompilerParams(vmem_limit_bytes=60 * MIB),
+        )(inverse, lengths[0, 0], held, query, keyval, w_out[0])
+
+    def packed():
+        return attend(table[0], land)
+
+    def whole():
+        arrived = pl.pallas_call(
+            whole_kernel,
+            name="whole",
+            out_shape=jax.ShapeDtypeStruct((groups, cap, blk, lanes), jnp.bfloat16),
+            in_specs=[smem, hbm],
+            out_specs=hbm,
+            scratch_shapes=[
+                pltpu.VMEM((pool_blocks, blk, lanes), jnp.bfloat16),
+                pltpu.VMEM((groups, cap, blk, lanes), jnp.bfloat16),
+                dma((15,)),
+                dma((15,)),
+                dma((2,)),
+            ],
+            compiler_params=pltpu.CompilerParams(
+                collective_id=2, has_side_effects=True, vmem_limit_bytes=60 * MIB
+            ),
+        )(send_index[0], old_pool)
+        hit = recv_slot[0].reshape(1, -1) == jnp.arange(blocks, dtype=jnp.int32)[:, None]
+        inverse = jnp.sum(jnp.where(hit, jnp.arange(groups * cap, dtype=jnp.int32)[None, :], 0), axis=1)
+        return attend(inverse, arrived.reshape(groups * cap, blk, lanes))
+
+    cache, part = lax.cond(over[0, 0] > 0, whole, packed)
 
     tp = lax.axis_size("tp")
     passed = pl.pallas_call(

time: 156 us -> 115 us (0.74)
  Pallas kernels: 142 us -> 111 us
  local copies, waits for them, and re-layouts: 11.6 us -> 1.91 us
    pallas_call x1, Pallas kernels: 106 us -> 77 us  [shards(): pl.pallas_call(move_kernel, name='move', out_shape=(jax.ShapeDtypeStruct(...]
    unnamed x17 -> x9, local copies, waits for them, and re-layouts: 10.9 us -> 0.72 us
    pallas_call x1, Pallas kernels: 13.9 us -> 8.92 us  [attend(): pl.pallas_call(attend_kernel, name='attend', out_shape=(jax.ShapeDtypeStr...]
    pallas_call x1, Pallas kernels: 22.5 us -> 24.7 us  [shards(): pl.pallas_call(sum_kernel, name='sum', out_shape=jax.ShapeDtypeStruct((re...]
where the time goes in v2:
time: 115 us
  Pallas kernels  111 us (97%)
  between operations  2.02 us (2%)
  local copies, waits for them, and re-layouts  1.91 us (2%)
    pallas_call x1, Pallas kernels, shards(): pl.pallas_call(move_kernel, name='move', out_shape=(jax.ShapeDtypeStruct(...  77 us
    pallas_call x1, Pallas kernels, shards(): pl.pallas_call(sum_kernel, name='sum', out_shape=jax.ShapeDtypeStruct((re...  24.7 us
    pallas_call x1, Pallas kernels, attend(): pl.pallas_call(attend_kernel, name='attend', out_shape=(jax.ShapeDtypeStr...  8.92 us

profile of v2, /device:TPU:1, one launch (start us, length us, event | category | flops | bytes accessed | tf_op | source)
XLA Modules:
  0.0 114.5 jit_solution(14095701249130613874)
XLA Ops:
  1.3 0.0 copy-start.1
  1.3 0.0 copy-start.2
  1.3 0.0 copy-start.3
  1.3 77.0 %move.1 = (bf16[508,32,256]{2,1,0:T(8,128)(2,1)}, f32[16,8,128]{2,1,0:T(8,128)S(1)}, bf16[16,256]{1,0:T(8,128)(2,1)S(1)}, s32[1,256]{1,0:T(1,128)S(1)}, s32[8,128]{1,0:T(8,128)}) custom-call(s32[16,32]{1,0:T(8,128)} %bitcast.24, s32[16,32]{1,0:T(8,128)} %bitcast.25, s32[1]{0:T(128)S(6)} %copy.17.holder, bf16[16,8192]{1,0:T(8,128)(2,1)} %bitcast.16, ...), custom_call_target="tpu_custom_call" | custom-call | tf_op jit(solution)/shard_map/move/pallas_call | solution.py:546
  78.3 1.2 %slice.3 = s32[1,1]{1,0:T(1,128)} slice(s32[8,128]{1,0:T(8,128)} %get-tuple-element.57), slice={[0:1], [0:1]} | slice | bytes 8 | tf_op jit(solution)/shard_map/slice | solution.py:635
  80.2 0.0 copy-done.1
  80.2 0.0 copy-done.2
  80.2 0.0 copy-done.3
  80.2 0.0 copy-start
  80.2 8.9 %conditional.1 = (f32[16,8192]{1,0:T(8,128)S(1)}, bf16[1,1,16,512,256]{4,3,2,1,0:T(8,128)(2,1)}) conditional(s32[]{:T(128)} %bitcast.14, (s32[1,256]{1,0:T(1,128)S(1)}, s32[1,1,16]{2,1,0:T(1,128)S(1)}, bf16[1,512,8192]{2,1,0:T(8,128)(2,1)}, bf16[508,32,256]{2,1,0:T(8,128)(2,1)}, f32[16,8,128]{2,1,0:T(8,128)S(1)}, ...), branch_computations={%region_0.0_spmd, %region_1.3_spmd} | conditional | flops 392960 | bytes 7184 | solution.py:635
  80.2 8.9 %attend.2 = (bf16[256,32,256]{2,1,0:T(8,128)(2,1)}, f32[16,8192]{1,0:T(8,128)S(1)}) custom-call(s32[256]{0:T(256)S(1)} %bitcast.29, s32[16]{0:T(128)S(1)} %bitcast.27, bf16[508,32,256]{2,1,0:T(8,128)(2,1)} %get-tuple-element.33.land, f32[16,8,128]{2,1,0:T(8,128)S(1)} %get-tuple-element.34.q, bf16[16,256]{1,0:T(8,128)(2,1)S(1)} %get-tuple-element.35.kv, ...), custom_call_target="tpu_custom_call" | custom-call | tf_op jit(solution)/shard_map/cond/branch_0_fun/attend/pallas_call | solution.py:592
  89.1 0.0 copy-done
  89.2 24.7 %sum.1 = bf16[16,8192]{1,0:T(8,128)(2,1)S(1)} custom-call(f32[16,8192]{1,0:T(8,128)S(1)} %get-tuple-element.62.part, bf16[16,8192]{1,0:T(8,128)(2,1)S(1)} %bitcast.17), custom_call_target="tpu_custom_call" | custom-call | tf_op jit(solution)/shard_map/sum/pallas_call | solution.py:638
  113.8 0.7 copy.18
Async XLA Ops:
  1.3 78.9 %copy-start.1 = (s32[1,16,32]{2,1,0:T(8,128)S(1)}, s32[1,16,32]{2,1,0:T(8,128)}, u32[]{:S(2)}) copy-start(s32[1,16,32]{2,1,0:T(8,128)} %param.19) | copy-start | bytes 6148
  1.3 78.9 %copy-start.2 = (s32[1,16,32]{2,1,0:T(8,128)S(1)}, s32[1,16,32]{2,1,0:T(8,128)}, u32[]{:S(2)}) copy-start(s32[1,16,32]{2,1,0:T(8,128)} %param.18) | copy-start | bytes 6148
  1.3 78.9 %copy-start.3 = (s32[1,1,16]{2,1,0:T(1,128)S(1)}, s32[1,1,16]{2,1,0:T(1,128)}, u32[]{:S(2)}) copy-start(s32[1,1,16]{2,1,0:T(1,128)} %param.21) | copy-start | bytes 196
  80.2 9.0 %copy-start = (bf16[1,1,16,8192]{3,2,1,0:T(8,128)(2,1)S(1)}, bf16[1,1,16,8192]{3,2,1,0:T(8,128)(2,1)}, u32[]{:S(2)}) copy-start(bf16[1,1,16,8192]{3,2,1,0:T(8,128)(2,1)} %param.12) | copy-start | bytes 786436

commit v3 on v2

--- a/solution.py
+++ b/solution.py
@@ -237,8 +237,9 @@
     kvsend, kvpeer, normed,
     send, recv, side_send, side_recv, mask_send, mask_recv, local,
 ):
-    y, z, _ = place()
+    y, z, tp = place()
     rep = lax.axis_index("rep")
+    count = lax.axis_size("tp")
     copies = [
         pltpu.make_async_copy(src, dst, local.at[i])
         for i, (src, dst) in enumerate(
@@ -253,12 +254,14 @@
     for d in FAR:
         for device in (at((y + d) % 4, z), at(y, (z + d) % 4)):
             pl.semaphore_signal(barrier, inc=1, device_id=device, device_id_type=MESH)
+    for k in range(1, count):
+        pl.semaphore_signal(barrier, inc=1, device_id={"tp": (tp + k) % count}, device_id_type=MESH)
 
     recv_in.wait()
     row, _ = grid(8, 128)
     slots = jnp.where(row < 4, pack_y(widen(ring_order(recv_v[...]))), 256.0)
     masks[z, y] = ones(slots < 255.5)
-    pl.semaphore_wait(barrier, 6)
+    pl.semaphore_wait(barrier, 6 + count - 1)
 
     hops = []
     for d in FAR:
@@ -278,19 +281,23 @@
 
     peer = {"rep": 1 - rep}
     hidden_in.wait()
-    to_peer = remote(hidden, hpeer, side_send, side_recv, 0, peer)
+    share = hidden.shape[1] // count
+    eighth = pl.ds(pl.multiple_of(tp * share, share), share)
+    to_peer = remote(hidden.at[:, eighth], hpeer.at[:, eighth], side_send, side_recv, 0, peer)
     to_peer.start()
 
     first, second, over = route(masks, y, z)
     one_first, one_second, two_first, two_second = offsets(first, second)
     sidx_in.wait()
     index = widen(ring_order(sidx_v[...]))
-    one_v[...] = first_tables(masks, index, first, one_first, one_second, y, z, pool.shape[0])
+    table = first_tables(masks, index, first, one_first, one_second, y, z, pool.shape[0])
+    row, _ = grid(16, 128)
+    one_v[...] = jnp.where(row == 4, jnp.broadcast_to(over, (16, 128)).astype(jnp.int32), table)
     one_in = pltpu.make_async_copy(one_v, one_s, local.at[7])
     one_in.start()
-    over_o[...] = jnp.broadcast_to(over, over_o.shape).astype(jnp.int32)
     pool_in.wait()
     one_in.wait()
+    over_o[0] = one_s[4, 0]
 
     def pack(dst, begin, count, src, table, line):
         unroll = 8 if count % 8 == 0 else 6
@@ -319,6 +326,14 @@
             started.append(copy)
     wkv_in.start()
     wq_in.start()
+    to_peer.wait_recv()
+    shared = []
+    for k in range(1, count):
+        copy = remote(
+            hpeer.at[:, eighth], hpeer.at[:, eighth], side_send, side_recv, 1 + k, {"tp": (tp + k) % count}
+        )
+        copy.start()
+        shared.append(copy)
     pack(mid.at[0], 0, STAY, pool, one_s, y)
     pack(mid.at[1], 0, STAY, pool, one_s, 8 + z)
 
@@ -328,7 +343,8 @@
     inv_o[...] = final_table(slots, first, two_first, two_second, y, z)
 
     gain_in.wait()
-    to_peer.wait_recv()
+    for copy in shared:
+        copy.wait_recv()
     width = hidden.shape[1]
     step = 1024
     rows = hidden.shape[0]
@@ -393,7 +409,7 @@
         )
         copy.start()
         keep.append(copy)
-    for copy in [to_peer, back, *started]:
+    for copy in [to_peer, back, *shared, *started]:
         copy.wait_send()
     for copy in relays:
         copy.wait_recv()
@@ -434,85 +450,86 @@
         copy.wait()
 
 
-def attend_kernel(inv, lengths, land, q, kv, w_h, cache, out, held, w, att, sems):
-    w_in = pltpu.make_async_copy(w_h, w, sems.at[0])
-    blocks = held.shape[0]
-
-    def fetch(i, _):
-        for u in range(8):
-            j = i * 8 + u
-            pltpu.make_async_copy(land.at[inv[j]], held.at[j], sems.at[1]).start()
+def attend_kernel(inv, lengths, land, q, kv, cache, out, held, att, ready, stored):
+    requests = q.shape[0]
+    per = held.shape[0] // requests
+
+    def part(b):
+        return pl.ds(b * per, per)
+
+    def fetch(b, _):
+        for u in range(per):
+            j = b * per + u
+            pltpu.make_async_copy(land.at[inv[j]], held.at[j], ready.at[b]).start()
         return 0
 
-    lax.fori_loop(0, blocks // 8, fetch, 0)
-    w_in.start()
-    pltpu.make_async_copy(land.at[pl.ds(0, blocks)], held, sems.at[1]).wait()
-
-    requests = q.shape[0]
-    per = blocks // requests
+    lax.fori_loop(0, requests, fetch, 0)
+
     row = lax.broadcasted_iota(jnp.int32, held.shape[1:], 0)
-
+    position = lax.broadcasted_iota(jnp.int32, (q.shape[1], CTX), 1)
+    stores = []
     for b in range(requests):
+        pltpu.make_async_copy(land.at[pl.ds(0, per)], held.at[part(b)], ready.at[b]).wait()
         length = lengths[b]
         j = b * per + length // BLK
-        held[j] = jnp.where(row == length % BLK, kv[b : b + 1, :].astype(jnp.float32), held[j].astype(jnp.float32)).astype(jnp.bfloat16)
-    store = pltpu.make_async_copy(held, cache, sems.at[2])
-    store.start()
-
-    position = lax.broadcasted_iota(jnp.int32, (q.shape[1], CTX), 1)
-
-    for b in range(requests):
+        fresh = jnp.broadcast_to(kv[b : b + 1, :].astype(jnp.float32), row.shape)
+        held[j] = jnp.where(row == length % BLK, fresh, held[j].astype(jnp.float32)).astype(jnp.bfloat16)
+        store = pltpu.make_async_copy(held.at[part(b)], cache.at[part(b)], stored.at[b])
+        store.start()
+        stores.append(store)
         keys = held[b * per : (b + 1) * per, :, 0:HD].reshape(CTX, HD)
         values = held[b * per : (b + 1) * per, :, HD : 2 * HD].reshape(CTX, HD)
         scores = lax.dot_general(
             q[b].astype(jnp.bfloat16), keys, (((1,), (1,)), ((), ())), preferred_element_type=jnp.float32
         ) * HD ** (-0.5)
-        valid = position <= lengths[b]
+        valid = position <= length
         expo = jnp.where(valid, jnp.exp(jnp.where(valid, scores, 0.0)), 0.0)
         weights = (expo / jnp.sum(expo, axis=1, keepdims=True)).astype(jnp.bfloat16)
         att[b] = jnp.dot(weights, values, preferred_element_type=jnp.float32)
 
-    heads = w.shape[0] // HD
-    attended = jnp.concatenate([att[:, h, :] for h in range(heads)], axis=1).astype(jnp.bfloat16)
-    w_in.wait()
-    step = 1024
-
-    def body(i, _):
-        cut = pl.ds(pl.multiple_of(i * step, step), step)
-        out[:, cut] = jnp.dot(attended, w[:, cut], preferred_element_type=jnp.float32)
-        return 0
-
-    lax.fori_loop(0, w.shape[1] // step, body, 0)
-    store.wait()
-
-
-def sum_kernel(part, hidden, out, land, mine, send, recv):
+    heads = out.shape[1] // HD
+    out[...] = jnp.concatenate([att[:, h, :] for h in range(heads)], axis=1).astype(jnp.bfloat16)
+    for store in stores:
+        store.wait()
+
+
+def finish_kernel(attended, hidden, w_h, out, w, part, land, mine, send, recv, loaded):
     tp = lax.axis_index("tp")
     section = lax.axis_index("section")
     sections = lax.axis_size("section")
     count = lax.axis_size("tp")
-    step = part.shape[1] // count
+    step = out.shape[1] // count
 
     def cut(t):
         return pl.ds(pl.multiple_of(t * step, step), step)
+
+    order = [*range(1, count), 0]
+    loads = {}
+    for k in order:
+        loads[k] = pltpu.make_async_copy(w_h.at[:, cut((tp + k) % count)], w.at[k], loaded.at[k])
+        loads[k].start()
 
     barrier = pltpu.get_barrier_semaphore()
     for k in range(1, count):
         pl.semaphore_signal(barrier, inc=1, device_id={"tp": (tp + k) % count}, device_id_type=MESH)
     before = {"section": (section + sections - 1) % sections}
     pl.semaphore_signal(barrier, inc=1, device_id=before, device_id_type=MESH)
-    pl.semaphore_wait(barrier, count)
 
     sums = []
-    for k in range(1, count):
-        t = (tp + k) % count
-        copy = remote(part.at[:, cut(t)], land.at[k - 1], send, recv, k - 1, {"tp": t})
-        copy.start()
-        sums.append(copy)
-    total = hidden[:, cut(tp)].astype(jnp.float32) + part[:, cut(tp)]
+    for k in order:
+        loads[k].wait()
+        chunk = jnp.dot(attended[...], w[k], preferred_element_type=jnp.float32)
+        if k:
+            part[k - 1] = chunk.astype(jnp.bfloat16)
+            if not sums:
+                pl.semaphore_wait(barrier, count)
+            copy = remote(part.at[k - 1], land.at[k - 1], send, recv, k - 1, {"tp": (tp + k) % count})
+            copy.start()
+            sums.append(copy)
+    total = hidden[:, cut(tp)].astype(jnp.float32) + chunk
     for k in range(1, count):
         sums[k - 1].wait_recv()
-        total = total + land[k - 1]
+        total = total + land[k - 1].astype(jnp.float32)
     mine[...] = total.astype(jnp.bfloat16)
     shift = remote(mine, out.at[:, cut(tp)], send, recv, count - 1, {"section": (section + 1) % sections})
     shift.start()
@@ -541,6 +558,7 @@
     smem = pl.BlockSpec(memory_space=pltpu.SMEM)
     hbm = pl.BlockSpec(memory_space=pl.ANY)
 
+    tp = lax.axis_size("tp")
     places = 2 * (STAY + 3 * CAP_TWO)
     dma = pltpu.SemaphoreType.DMA
     land, query, keyval, table, over = pl.pallas_call(
@@ -551,10 +569,10 @@
             jax.ShapeDtypeStruct((requests, 8, HD), jnp.float32),
             jax.ShapeDtypeStruct((requests, lanes), jnp.bfloat16),
             jax.ShapeDtypeStruct((1, blocks), jnp.int32),
-            jax.ShapeDtypeStruct((8, 128), jnp.int32),
+            jax.ShapeDtypeStruct((1,), jnp.int32),
         ),
         in_specs=[hbm, hbm, smem, hbm, hbm, hbm, hbm, hbm],
-        out_specs=(hbm, vmem, vmem, vmem, vmem),
+        out_specs=(hbm, vmem, vmem, vmem, smem),
         scratch_shapes=[
             pltpu.VMEM((groups, cap), jnp.int32),
             pltpu.VMEM((groups, cap), jnp.int32),
@@ -577,8 +595,8 @@
             pltpu.VMEM((2 * requests, width), jnp.bfloat16),
             dma((12,)),
             dma((12,)),
-            dma((2,)),
-            dma((2,)),
+            dma((tp + 1,)),
+            dma((tp + 1,)),
             dma((6,)),
             dma((6,)),
             dma((11,)),
@@ -594,18 +612,18 @@
             name="attend",
             out_shape=(
                 jax.ShapeDtypeStruct((blocks, blk, lanes), jnp.bfloat16),
-                jax.ShapeDtypeStruct((requests, width), jnp.float32),
+                jax.ShapeDtypeStruct((requests, heads * HD), jnp.bfloat16),
             ),
-            in_specs=[smem, smem, hbm, vmem, vmem, hbm],
+            in_specs=[smem, smem, hbm, vmem, vmem],
             out_specs=(hbm, vmem),
             scratch_shapes=[
                 pltpu.VMEM((blocks, blk, lanes), jnp.bfloat16),
-                pltpu.VMEM(w_out.shape[1:], jnp.bfloat16),
                 pltpu.VMEM((requests, 8, HD), jnp.float32),
-                dma((3,)),
+                dma((requests,)),
+                dma((requests,)),
             ],
             compiler_params=pltpu.CompilerParams(vmem_limit_bytes=60 * MIB),
-        )(inverse, lengths[0, 0], held, query, keyval, w_out[0])
+        )(inverse, lengths[0, 0], held, query, keyval)
 
     def packed():
         return attend(table[0], land)
@@ -632,25 +650,27 @@
         inverse = jnp.sum(jnp.where(hit, jnp.arange(groups * cap, dtype=jnp.int32)[None, :], 0), axis=1)
         return attend(inverse, arrived.reshape(groups * cap, blk, lanes))
 
-    cache, part = lax.cond(over[0, 0] > 0, whole, packed)
-
-    tp = lax.axis_size("tp")
+    cache, attended = lax.cond(over[0] > 0, whole, packed)
+
     passed = pl.pallas_call(
-        sum_kernel,
-        name="sum",
+        finish_kernel,
+        name="finish",
         out_shape=jax.ShapeDtypeStruct((requests, width), jnp.bfloat16),
-        in_specs=[vmem, vmem],
+        in_specs=[vmem, vmem, hbm],
         out_specs=vmem,
         scratch_shapes=[
-            pltpu.VMEM((tp - 1, requests, width // tp), jnp.float32),
+            pltpu.VMEM((tp, heads * HD, width // tp), jnp.bfloat16),
+            pltpu.VMEM((tp - 1, requests, width // tp), jnp.bfloat16),
+            pltpu.VMEM((tp - 1, requests, width // tp), jnp.bfloat16),
             pltpu.VMEM((requests, width // tp), jnp.bfloat16),
-            pltpu.SemaphoreType.DMA((2 * tp - 1,)),
-            pltpu.SemaphoreType.DMA((2 * tp - 1,)),
+            dma((2 * tp - 1,)),
+            dma((2 * tp - 1,)),
+            dma((tp,)),
         ],
         compiler_params=pltpu.CompilerParams(
-            collective_id=1, has_side_effects=True, vmem_limit_bytes=8 * MIB
+            collective_id=1, has_side_effects=True, vmem_limit_bytes=60 * MIB
         ),
-    )(part, state)
+    )(attended, state, w_out[0])
     return passed[None, None], cache.reshape(1, 1, requests, CTX, lanes)
 
 

time: 115 us -> 111 us (0.965)
  Pallas kernels: 111 us -> 107 us
    pallas_call x1, Pallas kernels: 24.7 us -> 22.2 us  [shards(): pl.pallas_call(finish_kernel, name='finish', out_shape=jax.ShapeDtypeStru...]
    slice x1 -> x0, local copies, waits for them, and re-layouts: 1.18 us -> none  [shards(): cache, part = lax.cond(over[0, 0] > 0, whole, packed)]
where the time goes in v3:
time: 111 us
  Pallas kernels  107 us (96%)
  between operations  2.04 us (2%)
  local copies, waits for them, and re-layouts  1.68 us (2%)
    pallas_call x1, Pallas kernels, shards(): pl.pallas_call(move_kernel, name='move', out_shape=(jax.ShapeDtypeStruct(...  76.8 us
    pallas_call x1, Pallas kernels, shards(): pl.pallas_call(finish_kernel, name='finish', out_shape=jax.ShapeDtypeStru...  22.2 us
    pallas_call x1, Pallas kernels, attend(): pl.pallas_call(attend_kernel, name='attend', out_shape=(jax.ShapeDtypeStr...  8.01 us

profile of v3, /device:TPU:1, one launch (start us, length us, event | category | flops | bytes accessed | tf_op | source)
XLA Modules:
  0.0 110.8 jit_solution(15129030374004128069)
XLA Ops:
  1.3 0.0 copy-start
  1.3 0.0 copy-start.1
  1.3 0.0 copy-start.2
  1.3 76.8 %move.1 = (bf16[508,32,256]{2,1,0:T(8,128)(2,1)}, f32[16,8,128]{2,1,0:T(8,128)S(1)}, bf16[16,256]{1,0:T(8,128)(2,1)S(1)}, s32[1,256]{1,0:T(1,128)S(1)}, s32[1]{0:T(128)}) custom-call(s32[16,32]{1,0:T(8,128)} %bitcast.22, s32[16,32]{1,0:T(8,128)} %bitcast.23, s32[1]{0:T(128)S(6)} %copy.17.holder, bf16[16,8192]{1,0:T(8,128)(2,1)} %bitcast.19, ...), custom_call_target="tpu_custom_call" | custom-call | tf_op jit(solution)/shard_map/move/pallas_call | solution.py:564
  78.8 0.0 copy-done
  78.8 0.0 copy-done.1
  78.8 0.0 copy-done.2
  78.8 8.0 %conditional.1 = (bf16[16,512]{1,0:T(8,128)(2,1)S(1)}, bf16[1,1,16,512,256]{4,3,2,1,0:T(8,128)(2,1)}) conditional(s32[]{:T(128)} %bitcast.12, (s32[1,256]{1,0:T(1,128)S(1)}, s32[1,1,16]{2,1,0:T(1,128)S(1)}, bf16[508,32,256]{2,1,0:T(8,128)(2,1)}, f32[16,8,128]{2,1,0:T(8,128)S(1)}, bf16[16,256]{1,0:T(8,128)(2,1)S(1)}) %tuple.27, ...), branch_computations={%region_0.0_spmd, %region_1.3_spmd} | conditional | flops 392960 | bytes 7184 | solution.py:653
  78.8 8.0 %attend.2 = (bf16[256,32,256]{2,1,0:T(8,128)(2,1)}, bf16[16,512]{1,0:T(8,128)(2,1)S(1)}) custom-call(s32[256]{0:T(256)S(1)} %bitcast.27, s32[16]{0:T(128)S(1)} %bitcast.25, bf16[508,32,256]{2,1,0:T(8,128)(2,1)} %get-tuple-element.29.land, f32[16,8,128]{2,1,0:T(8,128)S(1)} %get-tuple-element.30.q, bf16[16,256]{1,0:T(8,128)(2,1)S(1)} %get-tuple-element.31.kv), custom_call_target="tpu_custom_call" | custom-call | tf_op jit(solution)/shard_map/cond/branch_0_fun/attend/pallas_call | solution.py:610
  86.9 22.2 %finish.1 = bf16[16,8192]{1,0:T(8,128)(2,1)} custom-call(bf16[16,512]{1,0:T(8,128)(2,1)S(1)} %get-tuple-element.56.attended, bf16[16,8192]{1,0:T(8,128)(2,1)} %bitcast.20, bf16[512,8192]{1,0:T(8,128)(2,1)} %bitcast.17), custom_call_target="tpu_custom_call" | custom-call | tf_op jit(solution)/shard_map/finish/pallas_call | solution.py:655
  109.1 1.7 %copy.18 = bf16[1,1,16,8192]{3,2,1,0:T(8,128)(2,1)} copy(bf16[1,1,16,8192]{3,2,1,0:T(8,128)(2,1)} %bitcast.21) | data formatting | bytes 524288
Async XLA Ops:
  1.3 77.5 %copy-start = (s32[1,16,32]{2,1,0:T(8,128)S(1)}, s32[1,16,32]{2,1,0:T(8,128)}, u32[]{:S(2)}) copy-start(s32[1,16,32]{2,1,0:T(8,128)} %param.19) | copy-start | bytes 6148
  1.3 77.5 %copy-start.1 = (s32[1,16,32]{2,1,0:T(8,128)S(1)}, s32[1,16,32]{2,1,0:T(8,128)}, u32[]{:S(2)}) copy-start(s32[1,16,32]{2,1,0:T(8,128)} %param.18) | copy-start | bytes 6148
  1.3 77.5 %copy-start.2 = (s32[1,1,16]{2,1,0:T(1,128)S(1)}, s32[1,1,16]{2,1,0:T(1,128)}, u32[]{:S(2)}) copy-start(s32[1,1,16]{2,1,0:T(1,128)} %param.21) | copy-start | bytes 196

commit v4 on v3

--- a/solution.py
+++ b/solution.py
@@ -13,8 +13,8 @@
 MESH = pl.DeviceIdType.MESH
 MIB = 2**20
 FAR = (1, 3, 2)
-CAP_ONE = 42
-CAP_TWO = 42
+CAP_ONE = 41
+CAP_TWO = 41
 STAY = 128
 BALANCE = 0.01
 
@@ -230,12 +230,12 @@
     return jnp.clip(jnp.sum(found, axis=0, keepdims=True).astype(jnp.int32), 0, 2 * total - 1)
 
 
-def move_kernel(
-    recv_h, sidx_h, holder, hidden_h, gain_h, pool_h, wq_h, wkv_h,
-    fin, q_o, kv_o, inv_o, over_o,
-    recv_v, sidx_v, pool, masks, one_v, two_v, one_s, two_s, stage_one, mid, stage_two, wq, wkv, hidden, gain, hpeer,
-    kvsend, kvpeer, normed,
-    send, recv, side_send, side_recv, mask_send, mask_recv, local,
+def step_kernel(
+    recv_h, sidx_h, holder, lengths, hidden_h, gain_h, pool_h, wq_h, wkv_h, w_h,
+    cache, out, q_o, kv_o, over_o,
+    recv_v, sidx_v, pool, masks, one_v, two_v, inv_v, one_s, two_s, inv_s, stage_one, mid, stage_two, fin, held,
+    wq, wkv, w, hidden, gain, hpeer, kvsend, kvpeer, normed, att, part, paired, land, land_hidden, mate_in,
+    send, recv, side_send, side_recv, mask_send, mask_recv, tail_send, tail_recv, local,
 ):
     y, z, tp = place()
     rep = lax.axis_index("rep")
@@ -243,10 +243,10 @@
     copies = [
         pltpu.make_async_copy(src, dst, local.at[i])
         for i, (src, dst) in enumerate(
-            ((recv_h, recv_v), (sidx_h, sidx_v), (hidden_h, hidden), (pool_h, pool), (gain_h, gain), (wkv_h, wkv), (wq_h, wq))
+            ((recv_h, recv_v), (sidx_h, sidx_v), (hidden_h, hidden), (pool_h, pool), (gain_h, gain), (wkv_h, wkv), (wq_h, wq), (w_h, w))
         )
     ]
-    recv_in, sidx_in, hidden_in, pool_in, gain_in, wkv_in, wq_in = copies
+    recv_in, sidx_in, hidden_in, pool_in, gain_in, wkv_in, wq_in, w_in = copies
     for copy in copies[:5]:
         copy.start()
 
@@ -254,14 +254,13 @@
     for d in FAR:
         for device in (at((y + d) % 4, z), at(y, (z + d) % 4)):
             pl.semaphore_signal(barrier, inc=1, device_id=device, device_id_type=MESH)
-    for k in range(1, count):
-        pl.semaphore_signal(barrier, inc=1, device_id={"tp": (tp + k) % count}, device_id_type=MESH)
+    others = announce(barrier)
 
     recv_in.wait()
     row, _ = grid(8, 128)
     slots = jnp.where(row < 4, pack_y(widen(ring_order(recv_v[...]))), 256.0)
     masks[z, y] = ones(slots < 255.5)
-    pl.semaphore_wait(barrier, 6 + count - 1)
+    pl.semaphore_wait(barrier, 6 + others)
 
     hops = []
     for d in FAR:
@@ -285,6 +284,7 @@
     eighth = pl.ds(pl.multiple_of(tp * share, share), share)
     to_peer = remote(hidden.at[:, eighth], hpeer.at[:, eighth], side_send, side_recv, 0, peer)
     to_peer.start()
+    ahead = send_hidden(hidden, land_hidden, tail_send, tail_recv)
 
     first, second, over = route(masks, y, z)
     one_first, one_second, two_first, two_second = offsets(first, second)
@@ -293,14 +293,14 @@
     table = first_tables(masks, index, first, one_first, one_second, y, z, pool.shape[0])
     row, _ = grid(16, 128)
     one_v[...] = jnp.where(row == 4, jnp.broadcast_to(over, (16, 128)).astype(jnp.int32), table)
-    one_in = pltpu.make_async_copy(one_v, one_s, local.at[7])
+    one_in = pltpu.make_async_copy(one_v, one_s, local.at[8])
     one_in.start()
     pool_in.wait()
     one_in.wait()
     over_o[0] = one_s[4, 0]
 
     def pack(dst, begin, count, src, table, line):
-        unroll = 8 if count % 8 == 0 else 6
+        unroll = 8
 
         def body(i, _):
             for u in range(unroll):
@@ -309,6 +309,8 @@
             return 0
 
         lax.fori_loop(0, count // unroll, body, 0)
+        for p in range(count // unroll * unroll, count):
+            dst[begin + p] = src[table[line, p]]
 
     stay_one = STAY + 3 * CAP_ONE
     stay_two = STAY + 3 * CAP_TWO
@@ -326,6 +328,7 @@
             started.append(copy)
     wkv_in.start()
     wq_in.start()
+    w_in.start()
     to_peer.wait_recv()
     shared = []
     for k in range(1, count):
@@ -338,9 +341,11 @@
     pack(mid.at[1], 0, STAY, pool, one_s, 8 + z)
 
     two_v[...] = second_tables(first, second, one_first, one_second, two_first, two_second, y, z)
-    two_in = pltpu.make_async_copy(two_v, two_s, local.at[8])
+    two_in = pltpu.make_async_copy(two_v, two_s, local.at[9])
     two_in.start()
-    inv_o[...] = final_table(slots, first, two_first, two_second, y, z)
+    inv_v[...] = final_table(slots, first, two_first, two_second, y, z)
+    inv_in = pltpu.make_async_copy(inv_v, inv_s, local.at[10])
+    inv_in.start()
 
     gain_in.wait()
     for copy in shared:
@@ -392,30 +397,63 @@
     relays = []
     for d in FAR:
         for way, line, device in ((0, (z + d) % 4, at(y, (z + d) % 4)), (1, 8 + (y + d) % 4, at((y + d) % 4, z))):
-            begin = STAY + (d - 1) * CAP_TWO
-            pack(stage_two.at[way], begin, CAP_TWO, mid.at[way], two_s, line)
+            begin = (way * 3 + d - 1) * CAP_TWO
+            pack(stage_two, begin, CAP_TWO, mid.at[way], two_s, line)
             copy = remote(
-                stage_two.at[way, pl.ds(begin, CAP_TWO)],
-                fin.at[pl.ds(way * stay_two + begin, CAP_TWO)],
+                stage_two.at[pl.ds(begin, CAP_TWO)],
+                fin.at[pl.ds(way * stay_two + STAY + (d - 1) * CAP_TWO, CAP_TWO)],
                 send, recv, 6 + way * 3 + d - 1, device,
             )
             copy.start()
             relays.append(copy)
-    keep = []
     for way, line in ((0, z), (1, 8 + y)):
-        pack(stage_two.at[way], 0, STAY, mid.at[way], two_s, line)
-        copy = pltpu.make_async_copy(
-            stage_two.at[way, pl.ds(0, STAY)], fin.at[pl.ds(way * stay_two, STAY)], local.at[9 + way]
-        )
-        copy.start()
-        keep.append(copy)
+        pack(fin, way * stay_two, STAY, mid.at[way], two_s, line)
+    inv_in.wait()
+    w_in.wait()
     for copy in [to_peer, back, *shared, *started]:
         copy.wait_send()
     for copy in relays:
         copy.wait_recv()
+
+    per = held.shape[0] // rows
+    extra = 2 * stay_two
+    for b in range(rows):
+        length = lengths[b]
+        fin[extra + b] = renewed(fin[inv_s[0, b * per + length // BLK]], length, kv_o[b : b + 1, :])
+
+    def order(b, _):
+        changed = lengths[b] // BLK
+        for i in range(per):
+            source = jnp.where(changed == i, extra + b, inv_s[0, b * per + i])
+            held[b * per + i] = fin[source]
+        return 0
+
+    lax.fori_loop(0, rows, order, 0)
+    store = pltpu.make_async_copy(held, cache, local.at[11])
+    store.start()
+    for b in range(rows):
+        attention(held, q_o, lengths, att, b)
+    project(att, w, part)
+    summed(part, out, paired, land, land_hidden, mate_in, tail_send, tail_recv, ahead)
     for copy in relays:
         copy.wait_send()
-    for copy in keep:
+    store.wait()
+
+
+def hand_kernel(source, cache, held, read, written):
+    count = read.shape[0]
+    per = source.shape[0] // count
+    reads, writes = [], []
+    for i in range(count):
+        part = pl.ds(i * per, per)
+        reads.append(pltpu.make_async_copy(source.at[part], held.at[part], read.at[i]))
+        writes.append(pltpu.make_async_copy(held.at[part], cache.at[part], written.at[i]))
+    for copy in reads:
+        copy.start()
+    for one, other in zip(reads, writes, strict=True):
+        one.wait()
+        other.start()
+    for copy in writes:
         copy.wait()
 
 
@@ -450,11 +488,39 @@
         copy.wait()
 
 
-def attend_kernel(inv, lengths, land, q, kv, cache, out, held, att, ready, stored):
+def attention(held, q, lengths, att, b):
+    per = held.shape[0] // q.shape[0]
+    keys = held[b * per : (b + 1) * per, :, 0:HD].reshape(CTX, HD)
+    values = held[b * per : (b + 1) * per, :, HD : 2 * HD].reshape(CTX, HD)
+    scores = lax.dot_general(
+        q[b].astype(jnp.bfloat16), keys, (((1,), (1,)), ((), ())), preferred_element_type=jnp.float32
+    ) * HD ** (-0.5)
+    valid = lax.broadcasted_iota(jnp.int32, scores.shape, 1) <= lengths[b]
+    expo = jnp.where(valid, jnp.exp(jnp.where(valid, scores, 0.0)), 0.0)
+    weights = (expo / jnp.sum(expo, axis=1, keepdims=True)).astype(jnp.bfloat16)
+    att[b] = jnp.dot(weights, values, preferred_element_type=jnp.float32)
+
+
+def project(att, w, part):
+    heads = w.shape[0] // HD
+    attended = jnp.concatenate([att[:, h, :] for h in range(heads)], axis=1).astype(jnp.bfloat16)
+    step = part.shape[3]
+    for t in range(part.shape[0] * part.shape[1]):
+        chunk = jnp.dot(attended, w[:, t * step : (t + 1) * step], preferred_element_type=jnp.float32)
+        part[t % 2, t // 2] = chunk.astype(jnp.bfloat16)
+
+
+def renewed(block, length, fresh):
+    row, _ = grid(*block.shape)
+    fresh = jnp.broadcast_to(fresh.astype(jnp.float32), block.shape)
+    return jnp.where(row == length % BLK, fresh, block.astype(jnp.float32)).astype(jnp.bfloat16)
+
+
+def attend_kernel(inv, lengths, land, q, kv, w_h, cache, part, held, w, att, ready, stored, loaded):
     requests = q.shape[0]
     per = held.shape[0] // requests
 
-    def part(b):
+    def span(b):
         return pl.ds(b * per, per)
 
     def fetch(b, _):
@@ -464,85 +530,106 @@
         return 0
 
     lax.fori_loop(0, requests, fetch, 0)
-
-    row = lax.broadcasted_iota(jnp.int32, held.shape[1:], 0)
-    position = lax.broadcasted_iota(jnp.int32, (q.shape[1], CTX), 1)
+    w_in = pltpu.make_async_copy(w_h, w, loaded.at[0])
+    w_in.start()
     stores = []
     for b in range(requests):
-        pltpu.make_async_copy(land.at[pl.ds(0, per)], held.at[part(b)], ready.at[b]).wait()
+        pltpu.make_async_copy(land.at[pl.ds(0, per)], held.at[span(b)], ready.at[b]).wait()
         length = lengths[b]
         j = b * per + length // BLK
-        fresh = jnp.broadcast_to(kv[b : b + 1, :].astype(jnp.float32), row.shape)
-        held[j] = jnp.where(row == length % BLK, fresh, held[j].astype(jnp.float32)).astype(jnp.bfloat16)
-        store = pltpu.make_async_copy(held.at[part(b)], cache.at[part(b)], stored.at[b])
+        held[j] = renewed(held[j], length, kv[b : b + 1, :])
+        store = pltpu.make_async_copy(held.at[span(b)], cache.at[span(b)], stored.at[b])
         store.start()
         stores.append(store)
-        keys = held[b * per : (b + 1) * per, :, 0:HD].reshape(CTX, HD)
-        values = held[b * per : (b + 1) * per, :, HD : 2 * HD].reshape(CTX, HD)
-        scores = lax.dot_general(
-            q[b].astype(jnp.bfloat16), keys, (((1,), (1,)), ((), ())), preferred_element_type=jnp.float32
-        ) * HD ** (-0.5)
-        valid = position <= length
-        expo = jnp.where(valid, jnp.exp(jnp.where(valid, scores, 0.0)), 0.0)
-        weights = (expo / jnp.sum(expo, axis=1, keepdims=True)).astype(jnp.bfloat16)
-        att[b] = jnp.dot(weights, values, preferred_element_type=jnp.float32)
-
-    heads = out.shape[1] // HD
-    out[...] = jnp.concatenate([att[:, h, :] for h in range(heads)], axis=1).astype(jnp.bfloat16)
+        attention(held, q, lengths, att, b)
+    w_in.wait()
+    project(att, w, part)
     for store in stores:
         store.wait()
 
 
-def finish_kernel(attended, hidden, w_h, out, w, part, land, mine, send, recv, loaded):
+def summed(part, out, paired, land, land_hidden, mate_in, send, recv, arriving):
+    tp = lax.axis_index("tp")
+    section = lax.axis_index("section")
+    chips = part.shape[1]
+    step = part.shape[3]
+    core, chip = tp % 2, tp // 2
+    mate = {"tp": chip * 2 + 1 - core}
+    after = (section + 1) % lax.axis_size("section")
+
+    def cut(t):
+        return pl.ds(pl.multiple_of(t * step, step), step)
+
+    def along(d):
+        return ((chip + d) % chips) * 2 + core
+
+    swap = remote(part.at[1 - core], mate_in, send, recv, 0, mate)
+    swap.start()
+    swap.wait_recv()
+    sums = []
+    for d in (*FAR, 0):
+        x = (chip + d) % chips
+        both = part[core, x].astype(jnp.float32) + mate_in[x].astype(jnp.float32)
+        paired[d] = both.astype(jnp.bfloat16)
+        copy = remote(paired.at[d], land.at[d], send, recv, 2 + d, {"section": after, "tp": along(d)})
+        copy.start()
+        sums.append(copy)
+    arriving.wait_recv()
+    total = land_hidden[...].astype(jnp.float32)
+    for copy, d in zip(sums, (*FAR, 0), strict=True):
+        copy.wait_recv()
+        total = total + land[d].astype(jnp.float32)
+    out[:, cut(tp)] = total.astype(jnp.bfloat16)
+
+    spread = []
+    for d in FAR:
+        copy = remote(out.at[:, cut(tp)], out.at[:, cut(tp)], send, recv, 6 + d, {"tp": along(d)})
+        copy.start()
+        spread.append(copy)
+    passed = [remote(out.at[:, cut(tp)], out.at[:, cut(tp)], send, recv, 10, mate)]
+    passed[0].start()
+    for copy, d in zip(spread, FAR, strict=True):
+        copy.wait_recv()
+        t = along(chips - d)
+        onward = remote(out.at[:, cut(t)], out.at[:, cut(t)], send, recv, 10 + d, mate)
+        onward.start()
+        passed.append(onward)
+    for copy in passed:
+        copy.wait_recv()
+    for copy in [swap, arriving, *sums, *spread, *passed]:
+        copy.wait_send()
+
+
+def announce(barrier):
     tp = lax.axis_index("tp")
     section = lax.axis_index("section")
     sections = lax.axis_size("section")
     count = lax.axis_size("tp")
-    step = out.shape[1] // count
-
-    def cut(t):
-        return pl.ds(pl.multiple_of(t * step, step), step)
-
-    order = [*range(1, count), 0]
-    loads = {}
-    for k in order:
-        loads[k] = pltpu.make_async_copy(w_h.at[:, cut((tp + k) % count)], w.at[k], loaded.at[k])
-        loads[k].start()
-
-    barrier = pltpu.get_barrier_semaphore()
+    before = (section + sections - 1) % sections
+    for d in range(count // 2):
+        pl.semaphore_signal(
+            barrier, inc=1, device_id={"section": before, "tp": (tp + 2 * d) % count}, device_id_type=MESH
+        )
     for k in range(1, count):
         pl.semaphore_signal(barrier, inc=1, device_id={"tp": (tp + k) % count}, device_id_type=MESH)
-    before = {"section": (section + sections - 1) % sections}
-    pl.semaphore_signal(barrier, inc=1, device_id=before, device_id_type=MESH)
-
-    sums = []
-    for k in order:
-        loads[k].wait()
-        chunk = jnp.dot(attended[...], w[k], preferred_element_type=jnp.float32)
-        if k:
-            part[k - 1] = chunk.astype(jnp.bfloat16)
-            if not sums:
-                pl.semaphore_wait(barrier, count)
-            copy = remote(part.at[k - 1], land.at[k - 1], send, recv, k - 1, {"tp": (tp + k) % count})
-            copy.start()
-            sums.append(copy)
-    total = hidden[:, cut(tp)].astype(jnp.float32) + chunk
-    for k in range(1, count):
-        sums[k - 1].wait_recv()
-        total = total + land[k - 1].astype(jnp.float32)
-    mine[...] = total.astype(jnp.bfloat16)
-    shift = remote(mine, out.at[:, cut(tp)], send, recv, count - 1, {"section": (section + 1) % sections})
-    shift.start()
-    shift.wait_recv()
-    spread = []
-    for k in range(1, count):
-        copy = remote(out.at[:, cut(tp)], out.at[:, cut(tp)], send, recv, count + k - 1, {"tp": (tp + k) % count})
-        copy.start()
-        spread.append(copy)
-    for copy in spread:
-        copy.wait_recv()
-    for copy in [*sums, shift, *spread]:
-        copy.wait_send()
+    return count // 2 + count - 1
+
+
+def send_hidden(hidden, land_hidden, send, recv):
+    tp = lax.axis_index("tp")
+    step = land_hidden.shape[1]
+    after = (lax.axis_index("section") + 1) % lax.axis_size("section")
+    own = pl.ds(pl.multiple_of(tp * step, step), step)
+    ahead = remote(hidden.at[:, own], land_hidden, send, recv, 1, {"section": after})
+    ahead.start()
+    return ahead
+
+
+def finish_kernel(part, hidden, out, paired, land, land_hidden, mate_in, send, recv):
+    barrier = pltpu.get_barrier_semaphore()
+    pl.semaphore_wait(barrier, announce(barrier))
+    ahead = send_hidden(hidden, land_hidden, send, recv)
+    summed(part, out, paired, land, land_hidden, mate_in, send, recv, ahead)
 
 
 def shards(
@@ -559,19 +646,32 @@
     hbm = pl.BlockSpec(memory_space=pl.ANY)
 
     tp = lax.axis_size("tp")
-    places = 2 * (STAY + 3 * CAP_TWO)
+    chips = tp // 2
+    chunk = width // tp
     dma = pltpu.SemaphoreType.DMA
-    land, query, keyval, table, over = pl.pallas_call(
-        move_kernel,
-        name="move",
+    blocks_of = jax.ShapeDtypeStruct((blocks, blk, lanes), jnp.bfloat16)
+    rows_of = jax.ShapeDtypeStruct((requests, width), jnp.bfloat16)
+    tail = [
+        pltpu.VMEM((chips, requests, chunk), jnp.bfloat16),
+        pltpu.VMEM((chips, requests, chunk), jnp.bfloat16),
+        pltpu.VMEM((requests, chunk), jnp.bfloat16),
+        pltpu.VMEM((chips, requests, chunk), jnp.bfloat16),
+    ]
+
+    def params(limit, **more):
+        return pltpu.CompilerParams(vmem_limit_bytes=limit * MIB, **more)
+
+    quick_cache, quick_passed, query, keyval, over = pl.pallas_call(
+        step_kernel,
+        name="step",
         out_shape=(
-            jax.ShapeDtypeStruct((places, blk, lanes), jnp.bfloat16),
+            blocks_of,
+            rows_of,
             jax.ShapeDtypeStruct((requests, 8, HD), jnp.float32),
             jax.ShapeDtypeStruct((requests, lanes), jnp.bfloat16),
-            jax.ShapeDtypeStruct((1, blocks), jnp.int32),
             jax.ShapeDtypeStruct((1,), jnp.int32),
         ),
-        in_specs=[hbm, hbm, smem, hbm, hbm, hbm, hbm, hbm],
+        in_specs=[hbm, hbm, smem, smem, hbm, hbm, hbm, hbm, hbm, hbm],
         out_specs=(hbm, vmem, vmem, vmem, smem),
         scratch_shapes=[
             pltpu.VMEM((groups, cap), jnp.int32),
@@ -580,53 +680,53 @@
             pltpu.VMEM((4, 4, 8, 128), jnp.float32),
             pltpu.VMEM((16, 128), jnp.int32),
             pltpu.VMEM((16, 128), jnp.int32),
+            pltpu.VMEM((1, blocks), jnp.int32),
             pltpu.SMEM((16, 128), jnp.int32),
             pltpu.SMEM((16, 128), jnp.int32),
+            pltpu.SMEM((1, blocks), jnp.int32),
             pltpu.VMEM((6 * CAP_ONE, blk, lanes), jnp.bfloat16),
             pltpu.VMEM((2, STAY + 3 * CAP_ONE, blk, lanes), jnp.bfloat16),
-            pltpu.VMEM((2, STAY + 3 * CAP_TWO, blk, lanes), jnp.bfloat16),
+            pltpu.VMEM((6 * CAP_TWO, blk, lanes), jnp.bfloat16),
+            pltpu.VMEM((2 * (STAY + 3 * CAP_TWO) + requests, blk, lanes), jnp.bfloat16),
+            pltpu.VMEM((blocks, blk, lanes), jnp.bfloat16),
             pltpu.VMEM(w_query.shape[1:], jnp.bfloat16),
             pltpu.VMEM(w_keyval.shape[2:], jnp.bfloat16),
+            pltpu.VMEM(w_out.shape[1:], jnp.bfloat16),
             pltpu.VMEM((requests, width), jnp.bfloat16),
             pltpu.VMEM((1, width), jnp.float32),
             pltpu.VMEM((requests, width), jnp.bfloat16),
             pltpu.VMEM((requests, lanes), jnp.bfloat16),
             pltpu.VMEM((requests, lanes), jnp.bfloat16),
             pltpu.VMEM((2 * requests, width), jnp.bfloat16),
+            pltpu.VMEM((requests, 8, HD), jnp.float32),
+            pltpu.VMEM((2, chips, requests, chunk), jnp.bfloat16),
+            *tail,
             dma((12,)),
             dma((12,)),
             dma((tp + 1,)),
             dma((tp + 1,)),
             dma((6,)),
             dma((6,)),
-            dma((11,)),
+            dma((14,)),
+            dma((14,)),
+            dma((12,)),
         ],
-        compiler_params=pltpu.CompilerParams(
-            collective_id=0, has_side_effects=True, vmem_limit_bytes=60 * MIB
-        ),
-    )(recv_slot[0], send_index[0], holder, state, gain, old_pool, w_query[0], w_keyval[0, 0])
-
-    def attend(inverse, held):
-        return pl.pallas_call(
-            attend_kernel,
-            name="attend",
-            out_shape=(
-                jax.ShapeDtypeStruct((blocks, blk, lanes), jnp.bfloat16),
-                jax.ShapeDtypeStruct((requests, heads * HD), jnp.bfloat16),
-            ),
-            in_specs=[smem, smem, hbm, vmem, vmem],
-            out_specs=(hbm, vmem),
-            scratch_shapes=[
-                pltpu.VMEM((blocks, blk, lanes), jnp.bfloat16),
-                pltpu.VMEM((requests, 8, HD), jnp.float32),
-                dma((requests,)),
-                dma((requests,)),
-            ],
-            compiler_params=pltpu.CompilerParams(vmem_limit_bytes=60 * MIB),
-        )(inverse, lengths[0, 0], held, query, keyval)
-
-    def packed():
-        return attend(table[0], land)
+        compiler_params=params(62, collective_id=0, has_side_effects=True),
+    )(
+        recv_slot[0], send_index[0], holder, lengths[0, 0], state, gain, old_pool, w_query[0], w_keyval[0, 0], w_out[0]
+    )
+
+    def quick():
+        handed = pl.pallas_call(
+            hand_kernel,
+            name="hand",
+            out_shape=blocks_of,
+            in_specs=[hbm],
+            out_specs=hbm,
+            scratch_shapes=[pltpu.VMEM((blocks, blk, lanes), jnp.bfloat16), dma((16,)), dma((16,))],
+            compiler_params=params(60),
+        )(quick_cache)
+        return handed, quick_passed
 
     def whole():
         arrived = pl.pallas_call(
@@ -642,35 +742,38 @@
                 dma((15,)),
                 dma((2,)),
             ],
-            compiler_params=pltpu.CompilerParams(
-                collective_id=2, has_side_effects=True, vmem_limit_bytes=60 * MIB
-            ),
+            compiler_params=params(60, collective_id=2, has_side_effects=True),
         )(send_index[0], old_pool)
         hit = recv_slot[0].reshape(1, -1) == jnp.arange(blocks, dtype=jnp.int32)[:, None]
         inverse = jnp.sum(jnp.where(hit, jnp.arange(groups * cap, dtype=jnp.int32)[None, :], 0), axis=1)
-        return attend(inverse, arrived.reshape(groups * cap, blk, lanes))
-
-    cache, attended = lax.cond(over[0] > 0, whole, packed)
-
-    passed = pl.pallas_call(
-        finish_kernel,
-        name="finish",
-        out_shape=jax.ShapeDtypeStruct((requests, width), jnp.bfloat16),
-        in_specs=[vmem, vmem, hbm],
-        out_specs=vmem,
-        scratch_shapes=[
-            pltpu.VMEM((tp, heads * HD, width // tp), jnp.bfloat16),
-            pltpu.VMEM((tp - 1, requests, width // tp), jnp.bfloat16),
-            pltpu.VMEM((tp - 1, requests, width // tp), jnp.bfloat16),
-            pltpu.VMEM((requests, width // tp), jnp.bfloat16),
-            dma((2 * tp - 1,)),
-            dma((2 * tp - 1,)),
-            dma((tp,)),
-        ],
-        compiler_params=pltpu.CompilerParams(
-            collective_id=1, has_side_effects=True, vmem_limit_bytes=60 * MIB
-        ),
-    )(attended, state, w_out[0])
+        cache, part = pl.pallas_call(
+            attend_kernel,
+            name="attend",
+            out_shape=(blocks_of, jax.ShapeDtypeStruct((2, chips, requests, chunk), jnp.bfloat16)),
+            in_specs=[smem, smem, hbm, vmem, vmem, hbm],
+            out_specs=(hbm, vmem),
+            scratch_shapes=[
+                pltpu.VMEM((blocks, blk, lanes), jnp.bfloat16),
+                pltpu.VMEM(w_out.shape[1:], jnp.bfloat16),
+                pltpu.VMEM((requests, 8, HD), jnp.float32),
+                dma((requests,)),
+                dma((requests,)),
+                dma((1,)),
+            ],
+            compiler_params=params(60),
+        )(inverse, lengths[0, 0], arrived.reshape(groups * cap, blk, lanes), query, keyval, w_out[0])
+        passed = pl.pallas_call(
+            finish_kernel,
+            name="finish",
+            out_shape=rows_of,
+            in_specs=[vmem, vmem],
+            out_specs=vmem,
+            scratch_shapes=[*tail, dma((14,)), dma((14,))],
+            compiler_params=params(57, collective_id=1, has_side_effects=True),
+        )(part, state)
+        return cache, passed
+
+    cache, passed = lax.cond(over[0] > 0, whole, quick)
     return passed[None, None], cache.reshape(1, 1, requests, CTX, lanes)
 
 

time: 111 us -> 105 us (0.946)
  Pallas kernels: 107 us -> 102 us
    pallas_call x3 -> x2, Pallas kernels: 107 us -> 102 us  [the longest x1 97.8 us: shards(): pl.pallas_call(step_kernel, name='step', out_shape=(blocks_of, rows_of, j...]
where the time goes in v4:
time: 105 us; the launch traced here: 104 us
  Pallas kernels  102 us (97%)
  between operations  2.05 us (2%)
    pallas_call x1, Pallas kernels, shards(): pl.pallas_call(step_kernel, name='step', out_shape=(blocks_of, rows_of, j...  97.8 us
    pallas_call x1, Pallas kernels, quick(): pl.pallas_call(hand_kernel, name='hand', out_shape=blocks_of, in_specs=[h...  3.85 us

profile of v4, /device:TPU:1, one launch (start us, length us, event | category | flops | bytes accessed | tf_op | source)
XLA Modules:
  0.0 104.4 jit_solution(12497614136262037549)
XLA Ops:
  1.3 0.0 copy-start
  1.3 0.0 copy-start.1
  1.3 0.0 copy-start.2
  1.3 0.0 copy-start.3
  1.3 97.8 %step.1 = (bf16[256,32,256]{2,1,0:T(8,128)(2,1)}, bf16[16,8192]{1,0:T(8,128)(2,1)S(1)}, f32[16,8,128]{2,1,0:T(8,128)S(1)}, bf16[16,256]{1,0:T(8,128)(2,1)S(1)}, s32[1]{0:T(128)}) custom-call(s32[16,32]{1,0:T(8,128)} %bitcast.25, s32[16,32]{1,0:T(8,128)} %bitcast.26, s32[1]{0:T(128)S(6)} %copy.17.holder, s32[16]{0:T(128)} %bitcast.28, ...), custom_call_target="tpu_custom_call" | custom-call | tf_op jit(solution)/shard_map/step/pallas_call | solution.py:664
  99.8 0.0 copy-done
  99.8 0.0 copy-done.1
  99.8 0.0 copy-done.2
  99.8 0.0 copy-done.3
  99.8 3.9 %conditional.1 = (bf16[16,8192]{1,0:T(8,128)(2,1)S(1)}, bf16[1,1,16,512,256]{4,3,2,1,0:T(8,128)(2,1)}) conditional(s32[]{:T(128)} %bitcast.13, (bf16[256,32,256]{2,1,0:T(8,128)(2,1)}, bf16[16,8192]{1,0:T(8,128)(2,1)S(1)}) %tuple.18, (s32[1,16,32]{2,1,0:T(8,128)S(1)}, s32[1,1,16]{2,1,0:T(1,128)S(1)}, s32[1,16,32]{2,1,0:T(8,128)S(1)}, ...), branch_computations={%region_0.0_spmd, %region_1.3_spmd} | conditional | flops 392960 | bytes 7184 | solution.py:776
  99.8 3.9 %hand.1 = bf16[256,32,256]{2,1,0:T(8,128)(2,1)} custom-call(bf16[256,32,256]{2,1,0:T(8,128)(2,1)} %get-tuple-element.22.source), custom_call_target="tpu_custom_call" | custom-call | tf_op jit(solution)/shard_map/cond/branch_0_fun/hand/pallas_call | solution.py:720
  103.7 0.7 copy.18
Async XLA Ops:
  1.3 98.5 %copy-start = (bf16[1,1,16,8192]{3,2,1,0:T(8,128)(2,1)S(1)}, bf16[1,1,16,8192]{3,2,1,0:T(8,128)(2,1)}, u32[]{:S(2)}) copy-start(bf16[1,1,16,8192]{3,2,1,0:T(8,128)(2,1)} %param.12) | copy-start | bytes 786436
  1.3 98.5 %copy-start.1 = (s32[1,16,32]{2,1,0:T(8,128)S(1)}, s32[1,16,32]{2,1,0:T(8,128)}, u32[]{:S(2)}) copy-start(s32[1,16,32]{2,1,0:T(8,128)} %param.19) | copy-start | bytes 6148
  1.3 98.5 %copy-start.2 = (s32[1,16,32]{2,1,0:T(8,128)S(1)}, s32[1,16,32]{2,1,0:T(8,128)}, u32[]{:S(2)}) copy-start(s32[1,16,32]{2,1,0:T(8,128)} %param.18) | copy-start | bytes 6148
  1.3 98.5 %copy-start.3 = (s32[1,1,16]{2,1,0:T(1,128)S(1)}, s32[1,1,16]{2,1,0:T(1,128)}, u32[]{:S(2)}) copy-start(s32[1,1,16]{2,1,0:T(1,128)} %param.21) | copy-start | bytes 196

commit v5 on v4

--- a/solution.py
+++ b/solution.py
@@ -13,10 +13,15 @@
 MESH = pl.DeviceIdType.MESH
 MIB = 2**20
 FAR = (1, 3, 2)
+LONG = (2, 1, 3, 0)
+OTHERS = sorted(
+    ((dy, dz) for dy in range(4) for dz in range(4) if dy or dz),
+    key=lambda d: -(min(d[0], 4 - d[0]) + min(d[1], 4 - d[1])),
+)
 CAP_ONE = 41
 CAP_TWO = 41
 STAY = 128
-BALANCE = 0.01
+BALANCE = (0.016, 0.01, 0.006)
 
 
 def place():
@@ -117,9 +122,9 @@
         )
 
     share = jnp.full((16, 128), 0.5, jnp.float32)
-    for _ in range(4):
+    for pace in BALANCE:
         a1, b1, a2, b2 = loads(counts * share, counts - counts * share)
-        share = jnp.clip(share + BALANCE * (jnp.maximum(b1, b2) - jnp.maximum(a1, a2)), 0.0, 1.0)
+        share = jnp.clip(share + pace * (jnp.maximum(b1, b2) - jnp.maximum(a1, a2)), 0.0, 1.0)
     share = jnp.where(g == h, 1.0, share)
     first = jnp.floor(counts * share + 0.5)
     second = counts - first
@@ -233,8 +238,8 @@
 def step_kernel(
     recv_h, sidx_h, holder, lengths, hidden_h, gain_h, pool_h, wq_h, wkv_h, w_h,
     cache, out, q_o, kv_o, over_o,
-    recv_v, sidx_v, pool, masks, one_v, two_v, inv_v, one_s, two_s, inv_s, stage_one, mid, stage_two, fin, held,
-    wq, wkv, w, hidden, gain, hpeer, kvsend, kvpeer, normed, att, part, paired, land, land_hidden, mate_in,
+    recv_v, sidx_v, pool, masks, one_v, two_v, inv_v, one_s, two_s, inv_s, stage_one, mid, stage_two, fin, changed_blocks, held,
+    wq, wkv, w, hidden, gain, hpeer, kvsend, kvpeer, normed, att, give, kept, paired, land, land_hidden, mate_in,
     send, recv, side_send, side_recv, mask_send, mask_recv, tail_send, tail_recv, local,
 ):
     y, z, tp = place()
@@ -251,41 +256,33 @@
         copy.start()
 
     barrier = pltpu.get_barrier_semaphore()
-    for d in FAR:
-        for device in (at((y + d) % 4, z), at(y, (z + d) % 4)):
-            pl.semaphore_signal(barrier, inc=1, device_id=device, device_id_type=MESH)
     others = announce(barrier)
+    for dy, dz in OTHERS:
+        device = at((y + dy) % 4, (z + dz) % 4)
+        pl.semaphore_signal(barrier, inc=1, device_id=device, device_id_type=MESH)
 
     recv_in.wait()
     row, _ = grid(8, 128)
     slots = jnp.where(row < 4, pack_y(widen(ring_order(recv_v[...]))), 256.0)
     masks[z, y] = ones(slots < 255.5)
-    pl.semaphore_wait(barrier, 6 + others)
+    pl.semaphore_wait(barrier, len(OTHERS) + others)
 
     hops = []
-    for d in FAR:
-        copy = remote(masks.at[z, y], masks.at[z, y], mask_send, mask_recv, d - 1, at((y + d) % 4, z))
+    for k, (dy, dz) in enumerate(OTHERS):
+        device = at((y + dy) % 4, (z + dz) % 4)
+        copy = remote(masks.at[z, y], masks.at[z, y], mask_send, mask_recv, k, device)
         copy.start()
         hops.append(copy)
     for copy in hops:
         copy.wait_recv()
-    for d in FAR:
-        copy = remote(masks.at[z], masks.at[z], mask_send, mask_recv, 3 + d - 1, at(y, (z + d) % 4))
-        copy.start()
-        hops.append(copy)
-    for copy in hops[3:]:
-        copy.wait_recv()
-    for copy in hops:
-        copy.wait_send()
-
+
+    hidden_in.wait()
     peer = {"rep": 1 - rep}
-    hidden_in.wait()
     share = hidden.shape[1] // count
     eighth = pl.ds(pl.multiple_of(tp * share, share), share)
     to_peer = remote(hidden.at[:, eighth], hpeer.at[:, eighth], side_send, side_recv, 0, peer)
     to_peer.start()
     ahead = send_hidden(hidden, land_hidden, tail_send, tail_recv)
-
     first, second, over = route(masks, y, z)
     one_first, one_second, two_first, two_second = offsets(first, second)
     sidx_in.wait()
@@ -410,7 +407,7 @@
         pack(fin, way * stay_two, STAY, mid.at[way], two_s, line)
     inv_in.wait()
     w_in.wait()
-    for copy in [to_peer, back, *shared, *started]:
+    for copy in [to_peer, back, *hops, *shared, *started]:
         copy.wait_send()
     for copy in relays:
         copy.wait_recv()
@@ -419,7 +416,8 @@
     extra = 2 * stay_two
     for b in range(rows):
         length = lengths[b]
-        fin[extra + b] = renewed(fin[inv_s[0, b * per + length // BLK]], length, kv_o[b : b + 1, :])
+        changed_blocks[b] = renewed(fin[inv_s[0, b * per + length // BLK]], length, kv_o[b : b + 1, :])
+    fin[extra : extra + rows] = changed_blocks[...]
 
     def order(b, _):
         changed = lengths[b] // BLK
@@ -433,8 +431,8 @@
     store.start()
     for b in range(rows):
         attention(held, q_o, lengths, att, b)
-    project(att, w, part)
-    summed(part, out, paired, land, land_hidden, mate_in, tail_send, tail_recv, ahead)
+    attended = side_by_side(att, w.shape[0] // HD)
+    summed(attended, w, out, give, kept, paired, land, land_hidden, mate_in, tail_send, tail_recv, ahead)
     for copy in relays:
         copy.wait_send()
     store.wait()
@@ -501,13 +499,8 @@
     att[b] = jnp.dot(weights, values, preferred_element_type=jnp.float32)
 
 
-def project(att, w, part):
-    heads = w.shape[0] // HD
-    attended = jnp.concatenate([att[:, h, :] for h in range(heads)], axis=1).astype(jnp.bfloat16)
-    step = part.shape[3]
-    for t in range(part.shape[0] * part.shape[1]):
-        chunk = jnp.dot(attended, w[:, t * step : (t + 1) * step], preferred_element_type=jnp.float32)
-        part[t % 2, t // 2] = chunk.astype(jnp.bfloat16)
+def side_by_side(att, heads):
+    return jnp.concatenate([att[:, h, :] for h in range(heads)], axis=1).astype(jnp.bfloat16)
 
 
 def renewed(block, length, fresh):
@@ -516,7 +509,7 @@
     return jnp.where(row == length % BLK, fresh, block.astype(jnp.float32)).astype(jnp.bfloat16)
 
 
-def attend_kernel(inv, lengths, land, q, kv, w_h, cache, part, held, w, att, ready, stored, loaded):
+def attend_kernel(inv, lengths, land, q, kv, cache, out, held, att, ready, stored):
     requests = q.shape[0]
     per = held.shape[0] // requests
 
@@ -530,8 +523,6 @@
         return 0
 
     lax.fori_loop(0, requests, fetch, 0)
-    w_in = pltpu.make_async_copy(w_h, w, loaded.at[0])
-    w_in.start()
     stores = []
     for b in range(requests):
         pltpu.make_async_copy(land.at[pl.ds(0, per)], held.at[span(b)], ready.at[b]).wait()
@@ -542,17 +533,16 @@
         store.start()
         stores.append(store)
         attention(held, q, lengths, att, b)
-    w_in.wait()
-    project(att, w, part)
+    out[...] = side_by_side(att, out.shape[1] // HD)
     for store in stores:
         store.wait()
 
 
-def summed(part, out, paired, land, land_hidden, mate_in, send, recv, arriving):
+def summed(attended, w, out, give, own, paired, land, land_hidden, mate_in, send, recv, arriving):
     tp = lax.axis_index("tp")
     section = lax.axis_index("section")
-    chips = part.shape[1]
-    step = part.shape[3]
+    chips = give.shape[0]
+    step = give.shape[2]
     core, chip = tp % 2, tp // 2
     mate = {"tp": chip * 2 + 1 - core}
     after = (section + 1) % lax.axis_size("section")
@@ -563,40 +553,46 @@
     def along(d):
         return ((chip + d) % chips) * 2 + core
 
-    swap = remote(part.at[1 - core], mate_in, send, recv, 0, mate)
+    def term(t):
+        return jnp.dot(attended, w[:, cut(t)], preferred_element_type=jnp.float32)
+
+    for x in range(chips):
+        give[x] = term(x * 2 + 1 - core).astype(jnp.bfloat16)
+    swap = remote(give, mate_in, send, recv, 0, mate)
     swap.start()
+    for x in range(chips):
+        own[x] = term(x * 2 + core)
     swap.wait_recv()
     sums = []
-    for d in (*FAR, 0):
+    for d in LONG:
         x = (chip + d) % chips
-        both = part[core, x].astype(jnp.float32) + mate_in[x].astype(jnp.float32)
-        paired[d] = both.astype(jnp.bfloat16)
+        paired[d] = (own[x] + mate_in[x].astype(jnp.float32)).astype(jnp.bfloat16)
         copy = remote(paired.at[d], land.at[d], send, recv, 2 + d, {"section": after, "tp": along(d)})
         copy.start()
         sums.append(copy)
     arriving.wait_recv()
     total = land_hidden[...].astype(jnp.float32)
-    for copy, d in zip(sums, (*FAR, 0), strict=True):
+    for copy, d in zip(sums, LONG, strict=True):
         copy.wait_recv()
         total = total + land[d].astype(jnp.float32)
     out[:, cut(tp)] = total.astype(jnp.bfloat16)
 
-    spread = []
-    for d in FAR:
+    spread = {}
+    for d in LONG[:3]:
         copy = remote(out.at[:, cut(tp)], out.at[:, cut(tp)], send, recv, 6 + d, {"tp": along(d)})
         copy.start()
-        spread.append(copy)
+        spread[d] = copy
     passed = [remote(out.at[:, cut(tp)], out.at[:, cut(tp)], send, recv, 10, mate)]
     passed[0].start()
-    for copy, d in zip(spread, FAR, strict=True):
-        copy.wait_recv()
+    for d in FAR:
+        spread[d].wait_recv()
         t = along(chips - d)
         onward = remote(out.at[:, cut(t)], out.at[:, cut(t)], send, recv, 10 + d, mate)
         onward.start()
         passed.append(onward)
     for copy in passed:
         copy.wait_recv()
-    for copy in [swap, arriving, *sums, *spread, *passed]:
+    for copy in [swap, arriving, *sums, *spread.values(), *passed]:
         copy.wait_send()
 
 
@@ -625,11 +621,11 @@
     return ahead
 
 
-def finish_kernel(part, hidden, out, paired, land, land_hidden, mate_in, send, recv):
+def finish_kernel(attended, hidden, w, out, give, own, paired, land, land_hidden, mate_in, send, recv):
     barrier = pltpu.get_barrier_semaphore()
     pl.semaphore_wait(barrier, announce(barrier))
     ahead = send_hidden(hidden, land_hidden, send, recv)
-    summed(part, out, paired, land, land_hidden, mate_in, send, recv, ahead)
+    summed(attended[...], w, out, give, own, paired, land, land_hidden, mate_in, send, recv, ahead)
 
 
 def shards(
@@ -652,6 +648,8 @@
     blocks_of = jax.ShapeDtypeStruct((blocks, blk, lanes), jnp.bfloat16)
     rows_of = jax.ShapeDtypeStruct((requests, width), jnp.bfloat16)
     tail = [
+        pltpu.VMEM((chips, requests, chunk), jnp.bfloat16),
+        pltpu.VMEM((chips, requests, chunk), jnp.float32),
         pltpu.VMEM((chips, requests, chunk), jnp.bfloat16),
         pltpu.VMEM((chips, requests, chunk), jnp.bfloat16),
         pltpu.VMEM((requests, chunk), jnp.bfloat16),
@@ -688,6 +686,7 @@
             pltpu.VMEM((2, STAY + 3 * CAP_ONE, blk, lanes), jnp.bfloat16),
             pltpu.VMEM((6 * CAP_TWO, blk, lanes), jnp.bfloat16),
             pltpu.VMEM((2 * (STAY + 3 * CAP_TWO) + requests, blk, lanes), jnp.bfloat16),
+            pltpu.VMEM((requests, blk, lanes), jnp.bfloat16),
             pltpu.VMEM((blocks, blk, lanes), jnp.bfloat16),
             pltpu.VMEM(w_query.shape[1:], jnp.bfloat16),
             pltpu.VMEM(w_keyval.shape[2:], jnp.bfloat16),
@@ -699,14 +698,13 @@
             pltpu.VMEM((requests, lanes), jnp.bfloat16),
             pltpu.VMEM((2 * requests, width), jnp.bfloat16),
             pltpu.VMEM((requests, 8, HD), jnp.float32),
-            pltpu.VMEM((2, chips, requests, chunk), jnp.bfloat16),
             *tail,
             dma((12,)),
             dma((12,)),
             dma((tp + 1,)),
             dma((tp + 1,)),
-            dma((6,)),
-            dma((6,)),
+            dma((len(OTHERS),)),
+            dma((len(OTHERS),)),
             dma((14,)),
             dma((14,)),
             dma((12,)),
@@ -723,7 +721,7 @@
             out_shape=blocks_of,
             in_specs=[hbm],
             out_specs=hbm,
-            scratch_shapes=[pltpu.VMEM((blocks, blk, lanes), jnp.bfloat16), dma((16,)), dma((16,))],
+            scratch_shapes=[pltpu.VMEM((blocks, blk, lanes), jnp.bfloat16), dma((4,)), dma((4,))],
             compiler_params=params(60),
         )(quick_cache)
         return handed, quick_passed
@@ -746,31 +744,29 @@
         )(send_index[0], old_pool)
         hit = recv_slot[0].reshape(1, -1) == jnp.arange(blocks, dtype=jnp.int32)[:, None]
         inverse = jnp.sum(jnp.where(hit, jnp.arange(groups * cap, dtype=jnp.int32)[None, :], 0), axis=1)
-        cache, part = pl.pallas_call(
+        cache, attended = pl.pallas_call(
             attend_kernel,
             name="attend",
-            out_shape=(blocks_of, jax.ShapeDtypeStruct((2, chips, requests, chunk), jnp.bfloat16)),
-            in_specs=[smem, smem, hbm, vmem, vmem, hbm],
+            out_shape=(blocks_of, jax.ShapeDtypeStruct((requests, heads * HD), jnp.bfloat16)),
+            in_specs=[smem, smem, hbm, vmem, vmem],
             out_specs=(hbm, vmem),
             scratch_shapes=[
                 pltpu.VMEM((blocks, blk, lanes), jnp.bfloat16),
-                pltpu.VMEM(w_out.shape[1:], jnp.bfloat16),
                 pltpu.VMEM((requests, 8, HD), jnp.float32),
                 dma((requests,)),
                 dma((requests,)),
-                dma((1,)),
             ],
             compiler_params=params(60),
-        )(inverse, lengths[0, 0], arrived.reshape(groups * cap, blk, lanes), query, keyval, w_out[0])
+        )(inverse, lengths[0, 0], arrived.reshape(groups * cap, blk, lanes), query, keyval)
         passed = pl.pallas_call(
             finish_kernel,
             name="finish",
             out_shape=rows_of,
-            in_specs=[vmem, vmem],
+            in_specs=[vmem, vmem, vmem],
             out_specs=vmem,
             scratch_shapes=[*tail, dma((14,)), dma((14,))],
             compiler_params=params(57, collective_id=1, has_side_effects=True),
-        )(part, state)
+        )(attended, state, w_out[0])
         return cache, passed
 
     cache, passed = lax.cond(over[0] > 0, whole, quick)

time: 105 us -> 104 us (level)
  no operation moved by 1% of the time
where the time goes in v5:
time: 104 us
  Pallas kernels  101 us (97%)
  between operations  2.05 us (2%)
    pallas_call x1, Pallas kernels, shards(): pl.pallas_call(step_kernel, name='step', out_shape=(blocks_of, rows_of, j...  97.6 us
    pallas_call x1, Pallas kernels, quick(): pl.pallas_call(hand_kernel, name='hand', out_shape=blocks_of, in_specs=[h...  3.3 us

profile of v5, /device:TPU:1, one launch (start us, length us, event | category | flops | bytes accessed | tf_op | source)
XLA Modules:
  0.0 103.7 jit_solution(10950479746476358740)
XLA Ops:
  1.3 0.0 copy-start
  1.3 0.0 copy-start.1
  1.3 0.0 copy-start.2
  1.3 0.0 copy-start.3
  1.3 97.6 %step.1 = (bf16[256,32,256]{2,1,0:T(8,128)(2,1)}, bf16[16,8192]{1,0:T(8,128)(2,1)S(1)}, f32[16,8,128]{2,1,0:T(8,128)S(1)}, bf16[16,256]{1,0:T(8,128)(2,1)S(1)}, s32[1]{0:T(128)}) custom-call(s32[16,32]{1,0:T(8,128)} %bitcast.25, s32[16,32]{1,0:T(8,128)} %bitcast.26, s32[1]{0:T(128)S(6)} %copy.17.holder, s32[16]{0:T(128)} %bitcast.28, ...), custom_call_target="tpu_custom_call" | custom-call | tf_op jit(solution)/shard_map/step/pallas_call | solution.py:662
  99.7 0.0 copy-done
  99.7 0.0 copy-done.1
  99.7 0.0 copy-done.2
  99.7 0.0 copy-done.3
  99.7 3.3 %conditional.1 = (bf16[16,8192]{1,0:T(8,128)(2,1)S(1)}, bf16[1,1,16,512,256]{4,3,2,1,0:T(8,128)(2,1)}) conditional(s32[]{:T(128)} %bitcast.13, (bf16[256,32,256]{2,1,0:T(8,128)(2,1)}, bf16[16,8192]{1,0:T(8,128)(2,1)S(1)}) %tuple.18, (s32[1,16,32]{2,1,0:T(8,128)S(1)}, s32[1,1,16]{2,1,0:T(1,128)S(1)}, s32[1,16,32]{2,1,0:T(8,128)S(1)}, ...), branch_computations={%region_0.0_spmd, %region_1.3_spmd} | conditional | flops 392960 | bytes 7184 | solution.py:772
  99.7 3.3 %hand.1 = bf16[256,32,256]{2,1,0:T(8,128)(2,1)} custom-call(bf16[256,32,256]{2,1,0:T(8,128)(2,1)} %get-tuple-element.22.source), custom_call_target="tpu_custom_call" | custom-call | tf_op jit(solution)/shard_map/cond/branch_0_fun/hand/pallas_call | solution.py:718
  103.0 0.7 copy.18
Async XLA Ops:
  1.3 98.4 %copy-start = (bf16[1,1,16,8192]{3,2,1,0:T(8,128)(2,1)S(1)}, bf16[1,1,16,8192]{3,2,1,0:T(8,128)(2,1)}, u32[]{:S(2)}) copy-start(bf16[1,1,16,8192]{3,2,1,0:T(8,128)(2,1)} %param.12) | copy-start | bytes 786436
  1.3 98.4 %copy-start.1 = (s32[1,16,32]{2,1,0:T(8,128)S(1)}, s32[1,16,32]{2,1,0:T(8,128)}, u32[]{:S(2)}) copy-start(s32[1,16,32]{2,1,0:T(8,128)} %param.19) | copy-start | bytes 6148
  1.3 98.4 %copy-start.2 = (s32[1,16,32]{2,1,0:T(8,128)S(1)}, s32[1,16,32]{2,1,0:T(8,128)}, u32[]{:S(2)}) copy-start(s32[1,16,32]{2,1,0:T(8,128)} %param.18) | copy-start | bytes 6148
  1.3 98.4 %copy-start.3 = (s32[1,1,16]{2,1,0:T(1,128)S(1)}, s32[1,1,16]{2,1,0:T(1,128)}, u32[]{:S(2)}) copy-start(s32[1,1,16]{2,1,0:T(1,128)} %param.21) | copy-start | bytes 196

commit v6 on v5

--- a/solution.py
+++ b/solution.py
@@ -438,7 +438,7 @@
     store.wait()
 
 
-def hand_kernel(source, cache, held, read, written):
+def hand_kernel(source, passed, cache, out, held, read, written):
     count = read.shape[0]
     per = source.shape[0] // count
     reads, writes = [], []
@@ -446,11 +446,13 @@
         part = pl.ds(i * per, per)
         reads.append(pltpu.make_async_copy(source.at[part], held.at[part], read.at[i]))
         writes.append(pltpu.make_async_copy(held.at[part], cache.at[part], written.at[i]))
+    writes.append(pltpu.make_async_copy(passed, out, written.at[count]))
     for copy in reads:
         copy.start()
-    for one, other in zip(reads, writes, strict=True):
-        one.wait()
-        other.start()
+    writes[count].start()
+    for i in range(count):
+        reads[i].wait()
+        writes[i].start()
     for copy in writes:
         copy.wait()
 
@@ -714,17 +716,19 @@
         recv_slot[0], send_index[0], holder, lengths[0, 0], state, gain, old_pool, w_query[0], w_keyval[0, 0], w_out[0]
     )
 
-    def quick():
-        handed = pl.pallas_call(
+    def hand(cache, passed):
+        return pl.pallas_call(
             hand_kernel,
             name="hand",
-            out_shape=blocks_of,
-            in_specs=[hbm],
-            out_specs=hbm,
-            scratch_shapes=[pltpu.VMEM((blocks, blk, lanes), jnp.bfloat16), dma((4,)), dma((4,))],
+            out_shape=(blocks_of, rows_of),
+            in_specs=[hbm, vmem],
+            out_specs=(hbm, hbm),
+            scratch_shapes=[pltpu.VMEM((blocks, blk, lanes), jnp.bfloat16), dma((4,)), dma((5,))],
             compiler_params=params(60),
-        )(quick_cache)
-        return handed, quick_passed
+        )(cache, passed)
+
+    def quick():
+        return hand(quick_cache, quick_passed)
 
     def whole():
         arrived = pl.pallas_call(
@@ -767,7 +771,7 @@
             scratch_shapes=[*tail, dma((14,)), dma((14,))],
             compiler_params=params(57, collective_id=1, has_side_effects=True),
         )(attended, state, w_out[0])
-        return cache, passed
+        return hand(cache, passed)
 
     cache, passed = lax.cond(over[0] > 0, whole, quick)
     return passed[None, None], cache.reshape(1, 1, requests, CTX, lanes)

time: 104 us -> 103 us (level)
  no operation moved by 1% of the time
where the time goes in v6:
time: 103 us
  Pallas kernels  101 us (98%)
  between operations  2.03 us (2%)
    pallas_call x1, Pallas kernels, shards(): pl.pallas_call(step_kernel, name='step', out_shape=(blocks_of, rows_of, j...  97.6 us
    pallas_call x1, Pallas kernels, hand(): pl.pallas_call(hand_kernel, name='hand', out_shape=(blocks_of, rows_of),...  3.4 us

profile of v6, /device:TPU:1, one launch (start us, length us, event | category | flops | bytes accessed | tf_op | source)
XLA Modules:
  0.0 103.1 jit_solution(364815927137707326)
XLA Ops:
  1.3 0.0 copy-start
  1.3 0.0 copy-start.1
  1.3 0.0 copy-start.2
  1.3 0.0 copy-start.3
  1.3 97.6 %step.1 = (bf16[256,32,256]{2,1,0:T(8,128)(2,1)}, bf16[16,8192]{1,0:T(8,128)(2,1)S(1)}, f32[16,8,128]{2,1,0:T(8,128)S(1)}, bf16[16,256]{1,0:T(8,128)(2,1)S(1)}, s32[1]{0:T(128)}) custom-call(s32[16,32]{1,0:T(8,128)} %bitcast.22, s32[16,32]{1,0:T(8,128)} %bitcast.23, s32[1]{0:T(128)S(6)} %copy.16.holder, s32[16]{0:T(128)} %bitcast.25, ...), custom_call_target="tpu_custom_call" | custom-call | tf_op jit(solution)/shard_map/step/pallas_call | solution.py:664
  99.7 0.0 copy-done
  99.7 0.0 copy-done.1
  99.7 0.0 copy-done.2
  99.7 0.0 copy-done.3
  99.7 3.4 %conditional.1 = (bf16[256,32,256]{2,1,0:T(8,128)(2,1)}, bf16[1,1,16,8192]{3,2,1,0:T(8,128)(2,1)}) conditional(s32[]{:T(128)} %bitcast.13, (bf16[256,32,256]{2,1,0:T(8,128)(2,1)}, bf16[16,8192]{1,0:T(8,128)(2,1)S(1)}) %tuple.25, (s32[1,16,32]{2,1,0:T(8,128)S(1)}, s32[1,1,16]{2,1,0:T(1,128)S(1)}, s32[1,16,32]{2,1,0:T(8,128)S(1)}, ...), branch_computations={%region_0.0_spmd, %region_1.3_spmd} | conditional | flops 392960 | bytes 7184 | solution.py:776
  99.7 3.4 %hand.4 = (bf16[256,32,256]{2,1,0:T(8,128)(2,1)}, bf16[16,8192]{1,0:T(8,128)(2,1)}) custom-call(bf16[256,32,256]{2,1,0:T(8,128)(2,1)} %get-tuple-element.36.source, bf16[16,8192]{1,0:T(8,128)(2,1)S(1)} %get-tuple-element.37.passed), custom_call_target="tpu_custom_call" | custom-call | tf_op jit(solution)/shard_map/cond/branch_0_fun/hand/pallas_call | solution.py:720
Async XLA Ops:
  1.3 98.4 %copy-start = (bf16[1,1,16,8192]{3,2,1,0:T(8,128)(2,1)S(1)}, bf16[1,1,16,8192]{3,2,1,0:T(8,128)(2,1)}, u32[]{:S(2)}) copy-start(bf16[1,1,16,8192]{3,2,1,0:T(8,128)(2,1)} %param.12) | copy-start | bytes 786436
  1.3 98.4 %copy-start.1 = (s32[1,16,32]{2,1,0:T(8,128)S(1)}, s32[1,16,32]{2,1,0:T(8,128)}, u32[]{:S(2)}) copy-start(s32[1,16,32]{2,1,0:T(8,128)} %param.19) | copy-start | bytes 6148
  1.3 98.4 %copy-start.2 = (s32[1,16,32]{2,1,0:T(8,128)S(1)}, s32[1,16,32]{2,1,0:T(8,128)}, u32[]{:S(2)}) copy-start(s32[1,16,32]{2,1,0:T(8,128)} %param.18) | copy-start | bytes 6148
  1.3 98.4 %copy-start.3 = (s32[1,1,16]{2,1,0:T(1,128)S(1)}, s32[1,1,16]{2,1,0:T(1,128)}, u32[]{:S(2)}) copy-start(s32[1,1,16]{2,1,0:T(1,128)} %param.21) | copy-start | bytes 196
